TPU v7x, 256 devices: a whole 4x4x8 slice. The times are simulated.
256 devices in a mesh: ctx: 32 (over x, y, core), exp: 8 (over z).
Axes of the slice: x: 4, y: 4, z: 8, core: 2. Of those that a mesh axis runs over, the one named last changes fastest.
Arguments:
- queries: bfloat16 [16384, 4096], P('ctx', 'exp'), may hold values from -7 to 7
- key_value_stack: bfloat16 [16384, 2, 512], P('ctx'), may hold values from -6 to 6
- vertical_cols: int32 [128, 4], replicated, may hold values from -1 to 123, as said below
- slash_offsets: int32 [128, 2], replicated, may hold values from 0 to 2, as said below
- resid: bfloat16 [16384, 4096], P(('ctx', 'exp')), may hold values from -6 to 6
- norm_gain: float32 [4096], replicated, may hold values from 0.1 to 1.9
- expert_ids: int32 [16384, 8], P(('ctx', 'exp')), may hold values from 0 to 127, all different within a row; in each aligned block of 64 rows (0 to 63, 64 to 127, ...) at most 5 rows name the same one
- gate_weights: float32 [16384, 8], P(('ctx', 'exp')), may hold values from 0.05 to 1
- w_in: bfloat16 [256, 2048, 1536], P(('ctx', 'exp')), may hold values from -0.09375 to 0.09375
- w_out: bfloat16 [256, 768, 2048], P(('ctx', 'exp')), may hold values from -0.21875 to 0.21875
Outputs:
- mixed: bfloat16 [16384, 4096], P(('ctx', 'exp'))
Inputs may be any that keep to these rules, and one draw needn't show every extreme that they name: `vertical_cols`: rows of the first span's query blocks are all -1; every other entry of row i names a block of a span before block i's span (4 blocks a span). The query blocks of one span name at most 2 distinct blocks of any one other span, exactly 2 for some pair of spans. Entries of a row may repeat. slash_offsets[i, 0] is 0 for every query block i. `expert_ids`: in each aligned block of 64 rows no expert is named by more than 5 rows, a bound that some block reaches.
All inputs are finite; a program needn't handle non-finite values.
Results may differ from a plain program's by a relative error of at most 0.006.
Values may be sent and summed in bfloat16 or wider, within the bound.
A program may use at most 128 MiB of HBM per device.

v0:
```python
import jax
import jax.numpy as jnp
from jax import lax
from jax.sharding import PartitionSpec as P

D = 4096
QUERY_HEADS = 32
KEY_VALUE_HEADS = 4
HEAD_SIZE = 128
FF = 768
TOPK = 8
BLOCK_TOKENS = 128
NV = 4
NS = 2
SLASH_REACH = 3
VCAP = 2


def passed_along(block, axis, distance):
    devices = range(lax.axis_size(axis))
    route = [(i - distance, i) for i in devices if i - distance in devices]
    return lax.ppermute(block, axis, route)


def swapped(block, axis, apart):
    count = lax.axis_size(axis)
    route = []
    for low in range(count):
        high = low | 1 << apart
        if high != low and high < count:
            route += [(low, high), (high, low)]
    return lax.ppermute(block, axis, route)


def local(
    queries,
    key_value_stack,
    vertical_cols,
    slash_offsets,
    resid,
    norm_gain,
    expert_ids,
    gate_weights,
    w_in,
    w_out,
):
    n_ctx = lax.axis_size("ctx")
    n_exp = lax.axis_size("exp")
    my_ctx = lax.axis_index("ctx")
    my_exp = lax.axis_index("exp")
    span = queries.shape[0]
    blocks = span // BLOCK_TOKENS
    heads_dev = queries.shape[1] // HEAD_SIZE
    query_group_size = QUERY_HEADS // KEY_VALUE_HEADS
    window_width = NS + NV
    key_scale = HEAD_SIZE ** (-0.5)
    half = D // 2
    kv_head = my_exp * heads_dev // query_group_size
    own_kv = lax.dynamic_slice_in_dim(key_value_stack, kv_head * HEAD_SIZE, HEAD_SIZE, 2)
    key_value_blocks = own_kv.reshape(blocks, BLOCK_TOKENS, 2 * HEAD_SIZE)
    reach = SLASH_REACH - 1
    prev_tail = passed_along(key_value_blocks[blocks - reach :], "ctx", 1)
    extended = jnp.concatenate([prev_tail, key_value_blocks], axis=0)
    block_ids = jnp.arange(blocks, dtype=jnp.int32)
    first_block = my_ctx * blocks
    my_cols = lax.dynamic_slice_in_dim(vertical_cols, first_block, blocks, 0)
    my_offsets = lax.dynamic_slice_in_dim(slash_offsets, first_block, blocks, 0)
    clamped = jnp.maximum(my_cols, 0)
    requests = vertical_cols.reshape(n_ctx, blocks * NV)
    targets = first_block + block_ids
    need_out = jnp.any(requests[:, :, None] == targets[None, None, :], axis=1).astype(jnp.int32)
    rank_out = jnp.cumsum(need_out, axis=1) - need_out
    selector = (
        (need_out[:, None, :] > 0)
        & (rank_out[:, None, :] == jnp.arange(VCAP, dtype=jnp.int32)[None, :, None])
    ).astype(jnp.bfloat16)
    outgoing = jnp.einsum(
        "rsb,bkf->rskf", selector, key_value_blocks, preferred_element_type=jnp.float32
    ).astype(jnp.bfloat16)
    incoming = lax.all_to_all(outgoing, "ctx", split_axis=0, concat_axis=0, tiled=True)
    all_ids = jnp.arange(n_ctx * blocks, dtype=jnp.int32).reshape(n_ctx, blocks)
    need_in = jnp.any(my_cols.reshape(-1)[None, None, :] == all_ids[:, :, None], axis=2).astype(
        jnp.int32
    )
    rank_in = jnp.cumsum(need_in, axis=1) - need_in
    owners = clamped // blocks
    local_ids = clamped % blocks
    slots_in = rank_in[owners, local_ids]
    vertical = incoming.reshape(n_ctx * VCAP, BLOCK_TOKENS, 2 * HEAD_SIZE)[owners * VCAP + slots_in]
    global_ids = first_block + block_ids
    slash_ids = global_ids[:, None] - my_offsets
    slash_kv = extended[block_ids[:, None] - my_offsets + reach]
    in_slash = jnp.any(my_cols[:, :, None] == slash_ids[:, None, :], axis=2)
    earlier_mask = jnp.arange(NV)[None, :] < jnp.arange(NV)[:, None]
    repeated = jnp.any((my_cols[:, :, None] == my_cols[:, None, :]) & earlier_mask[None], axis=2)
    usable = jnp.concatenate([slash_ids >= 0, (my_cols >= 0) & ~in_slash & ~repeated], axis=1)
    gathered = jnp.concatenate([slash_kv, vertical], axis=1).reshape(
        blocks, window_width * BLOCK_TOKENS, 2 * HEAD_SIZE
    )
    key_row_slice = gathered[..., :HEAD_SIZE]
    value_rows = gathered[..., HEAD_SIZE:]
    query_blocks = queries.reshape(blocks, BLOCK_TOKENS, heads_dev, HEAD_SIZE)
    scores = (
        jnp.einsum(
            "qthd,qsd->qhts", query_blocks, key_row_slice, preferred_element_type=jnp.float32
        )
        * key_scale
    )
    row_pos = jnp.arange(BLOCK_TOKENS)
    col_pos = jnp.arange(window_width * BLOCK_TOKENS)
    causal = (col_pos[None, :] >= BLOCK_TOKENS) | (col_pos[None, :] <= row_pos[:, None])
    visible = jnp.repeat(usable, BLOCK_TOKENS, axis=1)[:, None, None, :] & causal[None, None, :, :]
    masked = jnp.where(visible, scores, -1e30)
    row_max = jnp.max(masked, axis=-1, keepdims=True)
    raw_weights = jnp.where(visible, jnp.exp(masked - row_max), 0.0)
    row_sum = jnp.sum(raw_weights, axis=-1, keepdims=True)
    probs = (raw_weights / row_sum).astype(jnp.bfloat16)
    attention = jnp.einsum("qhts,qsd->qthd", probs, value_rows, preferred_element_type=jnp.float32)
    attention = attention.astype(jnp.bfloat16).reshape(span, heads_dev * HEAD_SIZE)
    token_rows = lax.all_to_all(attention, "exp", split_axis=0, concat_axis=1, tiled=True)
    summed = resid.astype(jnp.float32) + token_rows.astype(jnp.float32)
    normed = (
        summed * lax.rsqrt(jnp.mean(summed * summed, axis=-1, keepdims=True) + 1e-06) * norm_gain
    ).astype(jnp.bfloat16)
    tok_count = resid.shape[0]
    experts = n_ctx * n_exp // 2
    capacity = max(2, (tok_count * TOPK * 5 + 4 * experts - 1) // (4 * experts))
    flat_ids = expert_ids.reshape(-1)
    onehot = (flat_ids[:, None] == jnp.arange(experts, dtype=jnp.int32)[None, :]).astype(jnp.int32)
    before = jnp.cumsum(onehot, axis=0) - onehot
    slots = jnp.sum(before * onehot, axis=1).reshape(tok_count, TOPK)
    shares = gate_weights / jnp.sum(gate_weights, axis=1, keepdims=True)
    routing = (
        expert_ids[None, None, :, :] == jnp.arange(experts, dtype=jnp.int32)[:, None, None, None]
    ) & (slots[None, None, :, :] == jnp.arange(capacity, dtype=jnp.int32)[None, :, None, None])
    routing = jnp.any(routing, axis=3).astype(jnp.bfloat16)
    outbound = jnp.einsum(
        "est,thd->ehsd",
        routing,
        normed.reshape(tok_count, 2, half),
        preferred_element_type=jnp.float32,
    ).astype(jnp.bfloat16)
    outbound = outbound.reshape(n_ctx, n_exp, capacity, half)
    received = lax.all_to_all(
        lax.all_to_all(outbound, "ctx", split_axis=0, concat_axis=0, tiled=True),
        "exp",
        split_axis=1,
        concat_axis=1,
        tiled=True,
    )
    expert_rows = received.reshape(-1, half)
    own_half = jnp.dot(expert_rows, w_in[0], preferred_element_type=jnp.float32).astype(
        jnp.bfloat16
    )
    theirs = swapped(own_half, "exp", 0)
    preact = own_half.astype(jnp.float32) + theirs.astype(jnp.float32)
    hidden = (jax.nn.silu(preact[:, :FF]) * preact[:, FF:]).astype(jnp.bfloat16)
    produced = jnp.dot(hidden, w_out[0], preferred_element_type=jnp.float32).astype(jnp.bfloat16)
    produced = produced.reshape(n_ctx, n_exp, capacity, half)
    returned = lax.all_to_all(
        lax.all_to_all(produced, "ctx", split_axis=0, concat_axis=0, tiled=True),
        "exp",
        split_axis=1,
        concat_axis=1,
        tiled=True,
    )
    results = returned.reshape(experts, 2, capacity, half)
    picked = results[expert_ids, :, slots].reshape(tok_count, TOPK, D)
    expert_sum = jnp.einsum("trd,tr->td", picked.astype(jnp.float32), shares)
    return (summed + expert_sum).astype(jnp.bfloat16)


def solution(mesh):
    in_specs = (
        P("ctx", "exp"),
        P("ctx", None, None),
        P(),
        P(),
        P(("ctx", "exp"), None),
        P(),
        P(("ctx", "exp"), None),
        P(("ctx", "exp"), None),
        P(("ctx", "exp"), None, None),
        P(("ctx", "exp"), None, None),
    )
    out_specs = P(("ctx", "exp"), None)
    return jax.shard_map(local, mesh=mesh, in_specs=in_specs, out_specs=out_specs, check_vma=False)
```

profile of v0, /device:TPU:1, one launch (start us, length us, event | category | flops | bytes accessed | tf_op | source)
XLA Modules:
  0.0 731.9 jit_solution(3353984861846772396)
XLA Ops:
  9.9 8.6 %all-to-all-start = ((bf16[32,2,128,256]{3,2,1,0:T(8,128)(2,1)}), bf16[32,2,128,256]{3,2,1,0:T(8,128)(2,1)}, u32[]{:S(2)}, u32[]{:S(2)}) async-start(bf16[32,2,128,256]{3,2,1,0:T(8,128)(2,1)} %copy.131), calls=%async_computation | async-start | bytes 8388608 | tf_op jit(solution)/shard_map/all_to_all | solution.py:80
  33.7 34.3 %collective-permute-done = bf16[2,128,256]{2,1,0:T(8,128)(2,1)} collective-permute-done((bf16[2,128,256]{2,1,0:T(8,128)(2,1)}, bf16[2,128,256]{2,1,0:T(8,128)(2,1)}, u32[]{:S(2)}, u32[]{:S(2)}) %collective-permute-start) | collective-permute-done | bytes 131104 | tf_op jit(solution)/shard_map/ppermute | solution.py:22
  88.4 8.4 %all-to-all-start.1 = ((bf16[8,64,512]{2,1,0:T(8,128)(2,1)}), bf16[8,64,512]{2,1,0:T(8,128)(2,1)}, u32[]{:S(2)}, u32[]{:S(2)}) async-start(bf16[8,64,512]{2,1,0:T(8,128)(2,1)} %all_to_all.26), calls=%async_computation.1 | async-start | bytes 1048576 | tf_op jit(solution)/shard_map/all_to_all | solution.py:120
  99.3 15.7 %all-to-all-done.1 = bf16[8,64,512]{2,1,0:T(8,128)(2,1)} async-done(((bf16[8,64,512]{2,1,0:T(8,128)(2,1)}), bf16[8,64,512]{2,1,0:T(8,128)(2,1)}, u32[]{:S(2)}, u32[]{:S(2)}) %all-to-all-start.1) | async-done | bytes 524320 | tf_op jit(solution)/shard_map/all_to_all | solution.py:120
  126.1 10.2 %copy.146 = bf16[128,2,5,2048]{3,1,0,2:T(2,128)(2,1)} copy(bf16[128,2,5,2048]{3,0,2,1:T(8,128)(2,1)} %convert_bitcast_fusion) | data formatting | bytes 10485760 | tf_op jit(solution)/shard_map/convert_element_type | solution.py:142
  136.4 8.7 %reshape.210 = bf16[32,8,5,2048]{3,1,0,2:T(8,128)(2,1)} reshape(bf16[128,2,5,2048]{3,1,0,2:T(2,128)(2,1)} %copy.146) | data formatting | bytes 10485760 | tf_op jit(solution)/shard_map/reshape | solution.py:143
  148.0 68.3 %all_to_all.38 = bf16[32,8,5,2048]{3,1,2,0:T(8,128)(2,1)S(1)} all-to-all(bf16[32,8,5,2048]{3,1,2,0:T(8,128)(2,1)S(1)} %copy.147), channel_id=1, replica_groups=mesh['ctx'=32,'exp'=8] {'ctx'}, dimensions={0} | all-to-all | bytes 10485760 | tf_op jit(solution)/shard_map/all_to_all | solution.py:145
  219.2 121.6 %all_to_all.39 = bf16[32,8,5,2048]{3,0,2,1:T(8,128)(2,1)S(1)} all-to-all(bf16[32,8,5,2048]{3,0,2,1:T(8,128)(2,1)S(1)} %copy.148), channel_id=1, replica_groups=mesh['ctx'=32,'exp'=8] {'exp'}, dimensions={1} | all-to-all | bytes 10485760 | tf_op jit(solution)/shard_map/all_to_all | solution.py:144
  340.8 6.4 copy.149
  347.1 10.0 %reshape.211 = bf16[1280,2048]{1,0:T(8,128)(2,1)} reshape(bf16[32,8,5,2048]{3,2,1,0:T(8,128)(2,1)} %copy.149) | data formatting | bytes 10485760 | tf_op jit(solution)/shard_map/reshape | solution.py:151
  357.1 12.0 %convolution_convert_fusion.1 = bf16[1280,1536]{1,0:T(8,128)(2,1)S(1)} fusion(bf16[1280,2048]{1,0:T(8,128)(2,1)} %reshape.211, bf16[1,2048,1536]{2,1,0:T(8,128)(2,1)} %param.18), kind=kOutput, calls=%fused_computation.7 | convolution fusion | flops 8055029760 | bytes 15466496 | tf_op jit(solution)/shard_map/dot_general | solution.py:152
  369.6 86.1 %collective-permute-done.1 = bf16[1280,1536]{1,0:T(8,128)(2,1)S(1)} collective-permute-done((bf16[1280,1536]{1,0:T(8,128)(2,1)S(1)}, bf16[1280,1536]{1,0:T(8,128)(2,1)S(1)}, u32[]{:S(2)}, u32[]{:S(2)}) %collective-permute-start.1) | collective-permute-done | bytes 3932192 | tf_op jit(solution)/shard_map/ppermute | solution.py:32
  456.8 6.1 convolution_convert_fusion
  463.0 9.7 %reshape.212 = bf16[32,8,5,2048]{3,2,1,0:T(8,128)(2,1)} reshape(bf16[1280,2048]{1,0:T(8,128)(2,1)} %convolution_convert_fusion) | data formatting | bytes 10485760 | tf_op jit(solution)/shard_map/reshape | solution.py:159
  472.7 8.8 %copy.150 = bf16[32,8,5,2048]{3,1,2,0:T(8,128)(2,1)S(1)} copy(bf16[32,8,5,2048]{3,2,1,0:T(8,128)(2,1)} %reshape.212) | data formatting | bytes 10485760 | tf_op jit(solution)/shard_map/reshape | solution.py:159
  481.5 66.4 %all_to_all.40 = bf16[32,8,5,2048]{3,1,2,0:T(8,128)(2,1)S(1)} all-to-all(bf16[32,8,5,2048]{3,1,2,0:T(8,128)(2,1)S(1)} %copy.150), channel_id=1, replica_groups=mesh['ctx'=32,'exp'=8] {'ctx'}, dimensions={0} | all-to-all | bytes 10485760 | tf_op jit(solution)/shard_map/all_to_all | solution.py:161
  548.0 5.2 copy.151
  553.2 4.9 all-to-all-start.5
  558.6 118.8 %all-to-all-done.5 = bf16[32,8,5,2048]{3,0,2,1:T(8,128)(2,1)} async-done(((bf16[32,8,5,2048]{3,0,2,1:T(8,128)(2,1)}), bf16[32,8,5,2048]{3,0,2,1:T(8,128)(2,1)}, u32[]{:S(2)}, u32[]{:S(2)}) %all-to-all-start.5) | async-done | bytes 5242912 | tf_op jit(solution)/shard_map/all_to_all | solution.py:160
  677.4 7.9 %copy.152 = bf16[32,8,5,2048]{3,1,0,2:T(8,128)(2,1)} copy(bf16[32,8,5,2048]{3,0,2,1:T(8,128)(2,1)} %all-to-all-done.5) | data formatting | bytes 10485760 | tf_op jit(solution)/shard_map/all_to_all | solution.py:160
  685.4 9.2 %reshape.213 = bf16[128,2,5,2048]{3,1,0,2:T(2,128)(2,1)} reshape(bf16[32,8,5,2048]{3,1,0,2:T(8,128)(2,1)} %copy.152) | data formatting | bytes 10485760 | tf_op jit(solution)/shard_map/reshape | solution.py:167
  694.6 8.4 %copy.157 = bf16[128,2,5,2048]{3,1,2,0:T(2,128)(2,1)} copy(bf16[128,2,5,2048]{3,1,0,2:T(2,128)(2,1)} %reshape.213) | data formatting | bytes 10485760 | tf_op jit(solution)/shard_map/reshape | solution.py:167
  703.0 15.9 %gather_fusion.3 = bf16[512,2,2048]{2,1,0:T(2,128)(2,1)} fusion(bf16[128,2,5,2048]{3,1,2,0:T(2,128)(2,1)} %copy.157, s32[512]{0:T(512)S(1)} %reshape.239), kind=kCustom, calls=%fused_computation.3 | custom fusion | bytes 8392704 | tf_op jit(solution)/shard_map/gather | solution.py:168
  719.0 7.8 %reshape.215 = bf16[64,8,4096]{2,1,0:T(8,128)(2,1)} reshape(bf16[512,2,2048]{2,1,0:T(2,128)(2,1)} %gather_fusion.3) | data formatting | bytes 8388608 | tf_op jit(solution)/shard_map/reshape | solution.py:168
  (123 shorter events, 71.6 us)
Async XLA Ops:
  0.0 456.8 %copy-start = (bf16[1,768,2048]{2,1,0:T(8,128)(2,1)S(1)}, bf16[1,768,2048]{2,1,0:T(8,128)(2,1)}, u32[]{:S(2)}) copy-start(bf16[1,768,2048]{2,1,0:T(8,128)(2,1)} %param.19) | copy-start | bytes 9437188
  3.1 6.8 copy-start.13
  3.9 6.0 copy-start.8
  9.9 62.1 %all-to-all-start = ((bf16[32,2,128,256]{3,2,1,0:T(8,128)(2,1)}), bf16[32,2,128,256]{3,2,1,0:T(8,128)(2,1)}, u32[]{:S(2)}, u32[]{:S(2)}) async-start(bf16[32,2,128,256]{3,2,1,0:T(8,128)(2,1)} %copy.131), calls=%async_computation | async-start | bytes 8388608 | tf_op jit(solution)/shard_map/all_to_all | solution.py:80
  20.4 47.6 %collective-permute-start = (bf16[2,128,256]{2,1,0:T(8,128)(2,1)}, bf16[2,128,256]{2,1,0:T(8,128)(2,1)}, u32[]{:S(2)}, u32[]{:S(2)}) collective-permute-start(bf16[2,128,256]{2,1,0:T(8,128)(2,1)} %slice.25), channel_id=1, source_target_pairs={{0,8},{8,16},{16,24},{24,32},{32,40},{40,48},{48,56},{56,64},{64,7... | collective-permute-start | bytes 393224 | tf_op jit(solution)/shard_map/ppermute | solution.py:22
  29.3 0.7 copy-start.5
  33.7 45.7 %copy-start.12 = (s32[128,5]{0,1:T(8,128)}, s32[128,5]{0,1:T(8,128)S(1)}, u32[]{:S(2)}) copy-start(s32[128,5]{0,1:T(8,128)S(1)} %reduce-window.9) | copy-start | bytes 7684
  75.8 3.6 copy-start.7
  82.8 14.1 %slice-start = ((s32[128,5]{0,1:T(8,128)}), s32[128,4]{0,1:T(4,128)S(1)}, s32[]{:S(2)}) async-start(s32[128,5]{0,1:T(8,128)} %copy-done.12), calls=%async_computation.6 | async-start | bytes 4096 | tf_op jit(solution)/shard_map/slice.1
  82.8 14.1 %copy-start.6 = (s32[128,4,128]{0,1,2:T(4,128)S(1)}, s32[128,4,128]{0,1,2:T(4,128)}, u32[]{:S(2)}) copy-start(s32[128,4,128]{0,1,2:T(4,128)} %copy-done.5) | copy-start | bytes 786436
  84.3 33.7 %copy-start.9 = (f32[4096]{0:T(1024)S(1)}, f32[4096]{0:T(1024)}, u32[]{:S(2)}) copy-start(f32[4096]{0:T(1024)} %param.15) | copy-start | bytes 49156
  88.4 26.5 %all-to-all-start.1 = ((bf16[8,64,512]{2,1,0:T(8,128)(2,1)}), bf16[8,64,512]{2,1,0:T(8,128)(2,1)}, u32[]{:S(2)}, u32[]{:S(2)}) async-start(bf16[8,64,512]{2,1,0:T(8,128)(2,1)} %all_to_all.26), calls=%async_computation.1 | async-start | bytes 1048576 | tf_op jit(solution)/shard_map/all_to_all | solution.py:120
  115.0 3.0 copy-start.3
  116.3 1.7 copy-start.1
  369.1 86.6 %collective-permute-start.1 = (bf16[1280,1536]{1,0:T(8,128)(2,1)S(1)}, bf16[1280,1536]{1,0:T(8,128)(2,1)S(1)}, u32[]{:S(2)}, u32[]{:S(2)}) collective-permute-start(bf16[1280,1536]{1,0:T(8,128)(2,1)S(1)} %convolution_convert_fusion.1), channel_id=1, source_target_pairs={{0,1},{1,0},{2,3},{3,2},{4,5},{5,4},{6,7},{7,6},{8,9},{9,8},{10,11... | collective-permute-start | bytes 11796488 | tf_op jit(solution)/shard_map/ppermute | solution.py:32
  553.2 5.1 copy-start.10
  553.2 5.3 copy-start.11
  553.2 124.2 %all-to-all-start.5 = ((bf16[32,8,5,2048]{3,0,2,1:T(8,128)(2,1)}), bf16[32,8,5,2048]{3,0,2,1:T(8,128)(2,1)}, u32[]{:S(2)}, u32[]{:S(2)}) async-start(bf16[32,8,5,2048]{3,0,2,1:T(8,128)(2,1)} %copy.151), calls=%async_computation.5 | async-start | bytes 10485760 | tf_op jit(solution)/shard_map/all_to_all | solution.py:160
  726.8 3.5 copy-start.2
  726.8 3.5 copy-start.4
where the time goes:
time: 741 us; the launch traced here: 732 us
  blocking collectives  256 us (35%)
  waiting for transfers between devices  255 us (34%)
  local copies, waits for them, and re-layouts  144 us (19%)
  matrix products  31.4 us (4%)
  starting transfers between devices  26 us (4%)
  other arithmetic  19.1 us (3%)
    all_to_all x1, blocking collectives, local(): lax.all_to_all(lax.all_to_all(outbound, 'ctx', split_axis=0, concat_axis=...  122 us
    all_to_all x1, waiting for transfers between devices, local(): lax.all_to_all(lax.all_to_all(produced, 'ctx', split_axis=0, concat_axis=...  119 us
    ppermute x1, waiting for transfers between devices, swapped(): return lax.ppermute(block, axis, route)  86.1 us
    all_to_all x1, blocking collectives, local(): lax.all_to_all(outbound, 'ctx', split_axis=0, concat_axis=0, tiled=True)  68.3 us
    all_to_all x1, blocking collectives, local(): lax.all_to_all(produced, 'ctx', split_axis=0, concat_axis=0, tiled=True)  66.4 us
    ppermute x1, waiting for transfers between devices, passed_along(): return lax.ppermute(block, axis, route)  34.3 us
    reshape x2, local copies, waits for them, and re-layouts, local(): produced = produced.reshape(n_ctx, n_exp, capacity, half)  18.6 us
    reshape x2, local copies, waits for them, and re-layouts, local(): results = returned.reshape(experts, 2, capacity, half)  17.7 us
  transfers between devices with their start and end apart: 5, of which 4 were waited for; matrix products, arithmetic and copies ran while one was open for 2% of the time, Pallas kernels for 0%

commit v1 on v0

v1 whole, which is shorter than its diff:
```python
import jax
import jax.numpy as jnp
from jax import lax
from jax.experimental import pallas as pl
from jax.experimental.pallas import tpu as pltpu
from jax.sharding import PartitionSpec as P

D = 4096
QUERY_HEADS = 32
KEY_VALUE_HEADS = 4
HEAD_SIZE = 128
FF = 768
TOPK = 8
BLOCK_TOKENS = 128
NV = 4
NS = 2
WINDOW = NS + NV

GRID = 4
CHIPS = GRID * GRID
PLANES = 8
TOK = 64
SPAN = PLANES * TOK
COLUMN = 2 * SPAN
CAP = 5
SLOTS = CAP * 2 * PLANES
GROUP = GRID * SLOTS
ROWS = CHIPS * SLOTS
HALF = D // 2
CHUNKS = 4
CHUNK = HALF // CHUNKS
MESH = pl.DeviceIdType.MESH
BF16 = jnp.bfloat16
F32 = jnp.float32


def attend_kernel(ids, usable, q_ref, *refs):
    kv, o_ref = refs[:WINDOW], refs[WINDOW]
    block = pl.program_id(0)
    heads = q_ref.shape[1] // HEAD_SIZE
    q = jnp.concatenate([q_ref[:, h * HEAD_SIZE : (h + 1) * HEAD_SIZE] for h in range(heads)], axis=0)
    keys = jnp.concatenate([kv[j][0, :, :HEAD_SIZE] for j in range(WINDOW)], axis=0)
    values = jnp.concatenate([kv[j][0, :, HEAD_SIZE:] for j in range(WINDOW)], axis=0)
    scores = lax.dot_general(q, keys, (((1,), (1,)), ((), ())), preferred_element_type=F32)
    scores = scores * HEAD_SIZE ** (-0.5)
    row = lax.broadcasted_iota(jnp.int32, (heads * BLOCK_TOKENS, BLOCK_TOKENS), 0) % BLOCK_TOKENS
    col = lax.broadcasted_iota(jnp.int32, (heads * BLOCK_TOKENS, BLOCK_TOKENS), 1)
    parts, masks = [], []
    for j in range(WINDOW):
        part = scores[:, j * BLOCK_TOKENS : (j + 1) * BLOCK_TOKENS]
        seen = jnp.full(part.shape, usable[block * WINDOW + j], jnp.int32) > 0
        if j == 0:
            seen = seen & (col <= row)
        parts.append(jnp.where(seen, part, -1e30))
        masks.append(seen)
    top = parts[0]
    for part in parts[1:]:
        top = jnp.maximum(top, part)
    top = jnp.max(top, axis=1, keepdims=True)
    parts = [jnp.where(seen, jnp.exp(part - top), 0.0) for part, seen in zip(parts, masks)]
    total = parts[0]
    for part in parts[1:]:
        total = total + part
    total = jnp.sum(total, axis=1, keepdims=True)
    probs = jnp.concatenate([(part / total).astype(BF16) for part in parts], axis=1)
    result = jnp.dot(probs, values, preferred_element_type=F32).astype(BF16)
    for h in range(heads):
        o_ref[:, h * HEAD_SIZE : (h + 1) * HEAD_SIZE] = result[h * BLOCK_TOKENS : (h + 1) * BLOCK_TOKENS]


def attend(queries, kv_blocks, ids, usable):
    blocks = queries.shape[0] // BLOCK_TOKENS
    width = queries.shape[1]

    def kv_spec(j):
        return pl.BlockSpec((1, BLOCK_TOKENS, 2 * HEAD_SIZE), lambda i, ids, usable: (ids[i * WINDOW + j], 0, 0))

    return pl.pallas_call(
        attend_kernel,
        grid_spec=pltpu.PrefetchScalarGridSpec(
            num_scalar_prefetch=2,
            grid=(blocks,),
            in_specs=[pl.BlockSpec((BLOCK_TOKENS, width), lambda i, ids, usable: (i, 0))]
            + [kv_spec(j) for j in range(WINDOW)],
            out_specs=pl.BlockSpec((BLOCK_TOKENS, width), lambda i, ids, usable: (i, 0)),
        ),
        out_shape=jax.ShapeDtypeStruct(queries.shape, BF16),
        compiler_params=pltpu.CompilerParams(vmem_limit_bytes=32 * 2**20),
        name="attend",
    )(ids, usable, queries, *([kv_blocks] * WINDOW))


def expert_kernel(
    attn, resid, gain, pos_in, pos_out, share_out, w_own, w_got, w_out, out,
    heads_in, gath, toks, hot, sent, rows, win, wout, mine, theirs, hid_out, hid, back, comb, sib, parts,
    a_s, a_r, r_s, r_r, l_s, l_r, c_s, c_r, d_s, d_r, p_s, p_r, h_s, h_r, o_s, o_r, u_s, u_r, z_s, z_r, w_s,
):
    ctx = lax.axis_index("ctx")
    z = lax.axis_index("exp")
    chip, c = lax.div(ctx, 2), lax.rem(ctx, 2)
    x, y = lax.div(chip, GRID), lax.rem(chip, GRID)
    sibling = chip * 2 + 1 - c
    mate = lax.div(z, 2) * 2 + 1 - lax.rem(z, 2)
    same = c == lax.rem(z, 2)
    apart = c != lax.rem(z, 2)

    def send(src, dst, s_sem, r_sem, to_ctx, to_z):
        return pltpu.make_async_remote_copy(
            src_ref=src, dst_ref=dst, send_sem=s_sem, recv_sem=r_sem,
            device_id=(to_ctx, to_z), device_id_type=MESH,
        )

    def loop(count, body):
        lax.fori_loop(0, count, lambda i, carry: (body(i), carry)[1], 0)

    def mod8(v):
        return lax.rem(v + 2 * PLANES, PLANES)

    barrier = pltpu.get_barrier_semaphore()

    def greet(cx, zz):
        pl.semaphore_signal(barrier, inc=1, device_id=(cx, zz), device_id_type=MESH)

    def greet_chip(d):
        @pl.when(d != chip)
        def _():
            greet(d * 2 + c, z)

    loop(CHIPS, greet_chip)
    loop(PLANES - 1, lambda r: greet(ctx, mod8(z + r + 1)))
    greet(sibling, z)
    greet(sibling, mate)

    def win_copy(ref, k):
        return pltpu.make_async_copy(ref.at[pl.ds(k * CHUNK, CHUNK), :], win.at[k], w_s.at[k])

    def wout_copy(k):
        return pltpu.make_async_copy(w_out.at[:, pl.ds(k * CHUNK, CHUNK)], wout.at[k], w_s.at[CHUNKS + k])

    for k in range(CHUNKS):
        @pl.when(same)
        def _():
            win_copy(w_own, k).start()

        @pl.when(apart)
        def _():
            win_copy(w_got, k).start()

        wout_copy(k).start()

    pl.semaphore_wait(barrier, (CHIPS - 1) + (PLANES - 1) + 2)

    def a_send(r):
        to = mod8(z + r + 1)
        return send(attn.at[pl.ds(pl.multiple_of(to * TOK, TOK), TOK), :], heads_in.at[z], a_s.at[to], a_r.at[z], ctx, to)

    loop(PLANES - 1, lambda r: a_send(r).start())
    heads_in[z] = attn[pl.ds(pl.multiple_of(z * TOK, TOK), TOK), :]

    def a_wait(r):
        src = mod8(z + r + 1)
        send(heads_in.at[src], heads_in.at[src], a_s.at[src], a_r.at[src], ctx, src).wait_recv()

    loop(PLANES - 1, a_wait)

    squares = jnp.zeros((TOK, 1), F32)
    for b in range(PLANES):
        summed = resid[:, b * CHUNK : (b + 1) * CHUNK].astype(F32) + heads_in[b].astype(F32)
        squares = squares + jnp.sum(summed * summed, axis=1, keepdims=True)
    scale = lax.rsqrt(squares / D + 1e-06)
    for b in range(PLANES):
        summed = resid[:, b * CHUNK : (b + 1) * CHUNK].astype(F32) + heads_in[b].astype(F32)
        gath[b % CHUNKS, z, b // CHUNKS] = (summed * scale * gain[:, b * CHUNK : (b + 1) * CHUNK]).astype(BF16)

    def piece(k, r, slot, half):
        return gath.at[k, slot] if r < 4 else gath.at[k, slot, half]

    def right(k, r):
        ref = piece(k, r, mod8(z - r + 1), 0)
        return send(ref, ref, r_s.at[k, r - 1], r_r.at[k, r - 1], ctx, mod8(z + 1))

    def left(k, r):
        ref = piece(k, r, mod8(z + r - 1), 1)
        return send(ref, ref, l_s.at[k, r - 1], l_r.at[k, r - 1], ctx, mod8(z - 1))

    def right_in(k, r):
        ref = piece(k, r, mod8(z - r), 0)
        return send(ref, ref, r_s.at[k, r - 1], r_r.at[k, r - 1], ctx, mod8(z + 1))

    def left_in(k, r):
        ref = piece(k, r, mod8(z + r), 1)
        return send(ref, ref, l_s.at[k, r - 1], l_r.at[k, r - 1], ctx, mod8(z - 1))

    def place(core, slot):
        return pl.ds(pl.multiple_of(core * SPAN + slot * TOK, TOK), TOK)

    def across(k, slot):
        return send(
            gath.at[k, slot, 1 - c], toks.at[k, place(c, slot), :], c_s.at[k, slot], c_r.at[k, slot], sibling, z
        )

    def across_in(k, slot):
        return send(
            gath.at[k, slot, 1 - c], toks.at[k, place(1 - c, slot), :], c_s.at[k, slot], c_r.at[k, slot], sibling, z
        )

    def arrived(k, slot):
        across(k, slot).start()
        toks[k, place(c, slot), :] = gath[k, slot, c]

    def d_send(k, d):
        at = pl.ds(pl.multiple_of(d * SLOTS, SLOTS), SLOTS)
        to = pl.ds(pl.multiple_of(chip * SLOTS, SLOTS), SLOTS)
        return send(sent.at[k, at, :], rows.at[k, to, :], d_s.at[k, d], d_r.at[k, chip], d * 2 + c, z)

    own = pl.ds(pl.multiple_of(chip * SLOTS, SLOTS), SLOTS)

    def dispatch(k):
        loop(PLANES, lambda s: across_in(k, s).wait_recv())

        def step(g):
            xd = lax.rem(x + g, GRID)
            slot = lax.broadcasted_iota(jnp.int32, (SLOTS, COLUMN), 0)
            for i in range(GRID):
                hot[i * SLOTS : (i + 1) * SLOTS, :] = jnp.where(slot == pos_in[xd * GRID + i], 1.0, 0.0).astype(BF16)
            at = pl.ds(pl.multiple_of(xd * GROUP, GROUP), GROUP)
            sent[k, at, :] = jnp.dot(hot[...], toks[k], preferred_element_type=F32).astype(BF16)
            for j in range(1, GRID):
                d_send(k, xd * GRID + lax.rem(y + j, GRID)).start()

            @pl.when(g > 0)
            def _():
                d_send(k, xd * GRID + y).start()

        loop(GRID, step)
        rows[k, own, :] = sent[k, own, :]

    for tick in range(1, 2 * CHUNKS + 4):
        for k in range(CHUNKS):
            r = tick - 2 * k
            if 2 <= r <= 5:
                right_in(k, r - 1).wait_recv()
                left_in(k, r - 1).wait_recv()
            if 1 <= r <= 4:
                right(k, r).start()
                left(k, r).start()
            if r == 1:
                arrived(k, z)
            if 2 <= r <= 4:
                arrived(k, mod8(z - r + 1))
                arrived(k, mod8(z + r - 1))
            if r == 5:
                arrived(k, mod8(z + 4))
        for k in range(CHUNKS):
            if tick - 2 * k == 5:
                dispatch(k)

    lane = lax.broadcasted_iota(jnp.int32, (HEAD_SIZE, ROWS), 1)
    owner = lax.broadcasted_iota(jnp.int32, (HEAD_SIZE, ROWS), 0) * SLOTS
    spread = jnp.where((lane >= owner) & (lane < owner + SLOTS), 1.0, 0.0).astype(BF16)

    def build(b):
        at = pl.ds(pl.multiple_of(b * 128, 128), 128)
        slot = jnp.dot(pos_out[at, :], spread, preferred_element_type=F32)
        share = jnp.dot(share_out[at, :], spread, preferred_element_type=F32)
        want = lax.rem(lax.broadcasted_iota(jnp.int32, (128, ROWS), 1), SLOTS).astype(F32)
        comb[at, :] = jnp.where(slot == want, share, 0.0).astype(BF16)

    loop(COLUMN // 128, build)

    for k in range(CHUNKS):
        win_copy(w_own, k).wait()
        wout_copy(k).wait()

    def span_of(g):
        xs = lax.rem(x - g + GRID, GRID)
        return xs, pl.ds(pl.multiple_of(xs * GROUP, GROUP), GROUP)

    def p_send(g):
        _, at = span_of(g)
        return send(mine.at[at, :], theirs.at[at, :], p_s.at[g], p_r.at[g], sibling, z)

    def first(g):
        xs, at = span_of(g)
        for i in range(GRID):
            src = xs * GRID + i

            @pl.when(src != chip)
            def _():
                for k in range(CHUNKS):
                    ref = rows.at[k, pl.ds(pl.multiple_of(src * SLOTS, SLOTS), SLOTS), :]
                    send(ref, ref, d_s.at[k, src], d_r.at[k, src], src * 2 + c, z).wait_recv()

        total = jnp.dot(rows[0, at, :], win[0], preferred_element_type=F32)
        for k in range(1, CHUNKS):
            total = total + jnp.dot(rows[k, at, :], win[k], preferred_element_type=F32)
        mine[at, :] = total.astype(BF16)
        p_send(g).start()

    loop(GRID, first)

    def h_send(g):
        _, at = span_of(g)
        return send(hid_out.at[at, :], hid.at[at, :], h_s.at[g], h_r.at[g], sibling, mate)

    def hidden(g):
        p_send(g).wait_recv()
        xs, _ = span_of(g)

        def part(i):
            at = pl.ds(pl.multiple_of(xs * GROUP + i * 32, 32), 32)
            pre = mine[at, :].astype(F32) + theirs[at, :].astype(F32)
            gate, up = pre[:, :FF], pre[:, FF:]
            value = (gate / (1.0 + jnp.exp(-gate)) * up).astype(BF16)

            @pl.when(same)
            def _():
                hid[at, :] = value

            @pl.when(apart)
            def _():
                hid_out[at, :] = value

        loop(GROUP // 32, part)

        @pl.when(apart)
        def _():
            h_send(g).start()

    loop(GRID, hidden)

    def d_done(k):
        def one(d):
            @pl.when(d != chip)
            def _():
                d_send(k, d).wait_send()

        loop(CHIPS, one)

    loop(CHUNKS, d_done)

    def o_send(n, d):
        at = pl.ds(pl.multiple_of(d * SLOTS, SLOTS), SLOTS)
        return send(sent.at[n, at, :], back.at[n, own, :], o_s.at[n, d], o_r.at[n, chip], d * 2 + c, z)

    def second(step):
        n, g = lax.div(step, GRID), lax.rem(step, GRID)
        xs, at = span_of(g)

        @pl.when((n == 0) & apart)
        def _():
            send(hid_out.at[at, :], hid.at[at, :], h_s.at[g], h_r.at[g], sibling, mate).wait_recv()

        sent[n, at, :] = jnp.dot(hid[at, :], wout[n], preferred_element_type=F32).astype(BF16)
        for j in range(1, GRID):
            o_send(n, xs * GRID + lax.rem(y + j, GRID)).start()

        @pl.when(g > 0)
        def _():
            o_send(n, xs * GRID + y).start()

        @pl.when(g == 0)
        def _():
            back[n, own, :] = sent[n, own, :]

    loop(CHUNKS * GRID, second)

    def ring_done(k):
        for r in range(1, 5):
            right(k, r).wait_send()
            left(k, r).wait_send()
        loop(PLANES, lambda s: across(k, s).wait_send())

    loop(CHUNKS, ring_done)

    def u_send(n):
        return send(toks.at[n, pl.ds(0, SPAN), :], sib.at[n], u_s.at[n], u_r.at[n], sibling, z)

    def z_send(n, to):
        return send(gath.at[n, to, 0], parts.at[n, z], z_s.at[n, to], z_r.at[n, z], ctx, to)

    def tokens_of(core):
        return pl.ds(pl.multiple_of(core * SPAN, SPAN), SPAN)

    def combine(step):
        @pl.when(step < CHUNKS)
        def _():
            n = step

            def one(d):
                @pl.when(d != chip)
                def _():
                    ref = back.at[n, pl.ds(pl.multiple_of(d * SLOTS, SLOTS), SLOTS), :]
                    send(ref, ref, o_s.at[n, d], o_r.at[n, d], d * 2 + c, z).wait_recv()

            loop(CHIPS, one)
            toks[n, pl.ds(0, SPAN), :] = jnp.dot(
                comb[tokens_of(1 - c), :], back[n], preferred_element_type=F32
            ).astype(BF16)
            u_send(n).start()

        @pl.when(step > 0)
        def _():
            n = step - 1
            total = jnp.dot(comb[tokens_of(c), :], back[n], preferred_element_type=F32)
            u_send(n).wait_recv()
            total = (total + sib[n].astype(F32)).astype(BF16)
            for s in range(PLANES):
                gath[n, s, 0] = total[s * TOK : (s + 1) * TOK]
            loop(PLANES - 1, lambda r: z_send(n, mod8(z + r + 1)).start())
            parts[n, z] = gath[n, z, 0]

    loop(CHUNKS + 1, combine)

    for n in range(CHUNKS):
        def one(r):
            src = mod8(z + r + 1)
            send(parts.at[n, src], parts.at[n, src], z_s.at[n, src], z_r.at[n, src], ctx, src).wait_recv()

        loop(PLANES - 1, one)
        for half in range(2):
            b = half * CHUNKS + n
            total = parts[n, half].astype(F32)
            for q in range(1, PLANES // 2):
                total = total + parts[n, 2 * q + half].astype(F32)
            summed = resid[:, b * CHUNK : (b + 1) * CHUNK].astype(F32) + heads_in[b].astype(F32)
            out[:, b * CHUNK : (b + 1) * CHUNK] = (summed + total).astype(BF16)

    loop(PLANES - 1, lambda r: a_send(r).wait_send())

    def last(g):
        p_send(g).wait_send()

        @pl.when(apart)
        def _():
            h_send(g).wait_send()

    loop(GRID, last)

    def left_all(n):
        def one(d):
            @pl.when(d != chip)
            def _():
                o_send(n, d).wait_send()

        loop(CHIPS, one)
        u_send(n).wait_send()
        loop(PLANES - 1, lambda r: z_send(n, mod8(z + r + 1)).wait_send())

    loop(CHUNKS, left_all)


def run_experts(attn, resid, gain, pos_in, pos_out, share_out, w_own, w_got, w_out):
    vmem = pl.BlockSpec(memory_space=pltpu.VMEM)
    hbm = pl.BlockSpec(memory_space=pl.ANY)
    dma = pltpu.SemaphoreType.DMA
    return pl.pallas_call(
        expert_kernel,
        out_shape=jax.ShapeDtypeStruct((TOK, D), BF16),
        in_specs=[vmem] * 6 + [hbm] * 3,
        out_specs=vmem,
        scratch_shapes=[
            pltpu.VMEM((PLANES, TOK, CHUNK), BF16),
            pltpu.VMEM((CHUNKS, PLANES, 2, TOK, CHUNK), BF16),
            pltpu.VMEM((CHUNKS, COLUMN, CHUNK), BF16),
            pltpu.VMEM((GROUP, COLUMN), BF16),
            pltpu.VMEM((CHUNKS, ROWS, CHUNK), BF16),
            pltpu.VMEM((CHUNKS, ROWS, CHUNK), BF16),
            pltpu.VMEM((CHUNKS, CHUNK, 2 * FF), BF16),
            pltpu.VMEM((CHUNKS, FF, CHUNK), BF16),
            pltpu.VMEM((ROWS, 2 * FF), BF16),
            pltpu.VMEM((ROWS, 2 * FF), BF16),
            pltpu.VMEM((ROWS, FF), BF16),
            pltpu.VMEM((ROWS, FF), BF16),
            pltpu.VMEM((CHUNKS, ROWS, CHUNK), BF16),
            pltpu.VMEM((COLUMN, ROWS), BF16),
            pltpu.VMEM((CHUNKS, SPAN, CHUNK), BF16),
            pltpu.VMEM((CHUNKS, PLANES, TOK, CHUNK), BF16),
            dma((PLANES,)), dma((PLANES,)),
            dma((CHUNKS, 4)), dma((CHUNKS, 4)),
            dma((CHUNKS, 4)), dma((CHUNKS, 4)),
            dma((CHUNKS, PLANES)), dma((CHUNKS, PLANES)),
            dma((CHUNKS, CHIPS)), dma((CHUNKS, CHIPS)),
            dma((GRID,)), dma((GRID,)),
            dma((GRID,)), dma((GRID,)),
            dma((CHUNKS, CHIPS)), dma((CHUNKS, CHIPS)),
            dma((CHUNKS,)), dma((CHUNKS,)),
            dma((CHUNKS, PLANES)), dma((CHUNKS, PLANES)),
            dma((2 * CHUNKS,)),
        ],
        compiler_params=pltpu.CompilerParams(
            collective_id=0, has_side_effects=True, vmem_limit_bytes=62 * 2**20
        ),
        cost_estimate=pl.CostEstimate(flops=25 * 10**9, bytes_accessed=12 * 10**6, transcendentals=10**6),
        name="experts",
    )(attn, resid, gain, pos_in, pos_out, share_out, w_own, w_got, w_out)


def local(
    queries, key_value_stack, vertical_cols, slash_offsets, resid,
    norm_gain, expert_ids, gate_weights, w_in, w_out,
):
    n_ctx = lax.axis_size("ctx")
    ctx = lax.axis_index("ctx")
    z = lax.axis_index("exp")
    core = ctx % 2
    blocks = queries.shape[0] // BLOCK_TOKENS
    heads_dev = queries.shape[1] // HEAD_SIZE

    kv_head = z * heads_dev // (QUERY_HEADS // KEY_VALUE_HEADS)
    own_kv = lax.dynamic_slice_in_dim(key_value_stack, kv_head * HEAD_SIZE, HEAD_SIZE, 2)
    own_kv = own_kv.reshape(blocks, BLOCK_TOKENS, 2 * HEAD_SIZE)
    kv_blocks = lax.all_gather(own_kv, "ctx", axis=0, tiled=True)

    route = []
    for i in range(n_ctx):
        for j in range(PLANES):
            if i % 2 != j % 2:
                route.append((i * PLANES + j, (i ^ 1) * PLANES + (j ^ 1)))
    w_own = w_in[0]
    w_got = lax.ppermute(w_own, ("ctx", "exp"), route)

    shares = gate_weights / jnp.sum(gate_weights, axis=1, keepdims=True)
    routing = jnp.concatenate([expert_ids.astype(F32), shares], axis=1)
    routing = lax.all_gather(routing, "exp", axis=0, tiled=True)
    other = lax.ppermute(routing, "ctx", [(i, i ^ 1) for i in range(n_ctx)])
    routing = jnp.where(
        core == 0, jnp.concatenate([routing, other], axis=0), jnp.concatenate([other, routing], axis=0)
    )
    ids = routing[:, :TOPK].astype(jnp.int32).T
    named = ids[None, :, :] == (jnp.arange(n_ctx, dtype=jnp.int32) * (PLANES // 2) + z // 2)[:, None, None]
    share = jnp.sum(jnp.where(named, routing[:, TOPK:].T[None], 0.0), axis=1)
    member = jnp.any(named, axis=1)
    upper = (jnp.arange(COLUMN)[:, None] < jnp.arange(COLUMN)[None, :]).astype(BF16)
    rank = jnp.dot(member.astype(BF16), upper, preferred_element_type=F32)
    pos = jnp.where(member, rank, -1.0).reshape(CHIPS, 2, COLUMN)
    share = share.reshape(CHIPS, 2, COLUMN)
    pos_in = lax.dynamic_slice_in_dim(pos, z % 2, 1, 1).astype(jnp.int32)
    pos_out = lax.dynamic_slice_in_dim(pos, core, 1, 1)[:, 0].T
    share_out = lax.dynamic_slice_in_dim(share, core, 1, 1)[:, 0].T
    pad = ((0, 0), (0, HEAD_SIZE - CHIPS))
    pos_out = jnp.pad(pos_out.astype(BF16), pad)
    share_out = jnp.pad(share_out.astype(BF16), pad)

    first = ctx * blocks
    cols = lax.dynamic_slice_in_dim(vertical_cols, first, blocks, 0)
    offsets = lax.dynamic_slice_in_dim(slash_offsets, first, blocks, 0)
    slash = (first + jnp.arange(blocks, dtype=jnp.int32))[:, None] - offsets
    in_slash = jnp.any(cols[:, :, None] == slash[:, None, :], axis=2)
    earlier = jnp.arange(NV)[None, :] < jnp.arange(NV)[:, None]
    repeated = jnp.any((cols[:, :, None] == cols[:, None, :]) & earlier[None], axis=2)
    usable = jnp.concatenate([slash >= 0, (cols >= 0) & ~in_slash & ~repeated], axis=1)
    chosen = jnp.maximum(jnp.concatenate([slash, cols], axis=1), 0)
    attn = attend(queries, kv_blocks, chosen.reshape(-1), usable.astype(jnp.int32).reshape(-1))

    return run_experts(attn, resid, norm_gain[None, :], pos_in, pos_out, share_out, w_own, w_got, w_out[0])


def solution(mesh):
    in_specs = (
        P("ctx", "exp"),
        P("ctx", None, None),
        P(),
        P(),
        P(("ctx", "exp"), None),
        P(),
        P(("ctx", "exp"), None),
        P(("ctx", "exp"), None),
        P(("ctx", "exp"), None, None),
        P(("ctx", "exp"), None, None),
    )
    out_specs = P(("ctx", "exp"), None)
    return jax.shard_map(local, mesh=mesh, in_specs=in_specs, out_specs=out_specs, check_vma=False)
```

time: 741 us -> 349 us (0.47); the launches traced: 732 us -> 348 us
  waiting for transfers between devices: 255 us -> 0.02 us
  Pallas kernels: 0 us -> 223 us
  blocking collectives: 256 us -> 83.3 us
  local copies, waits for them, and re-layouts: 144 us -> 12.5 us
  matrix products: 31.4 us -> 0.36 us
  other arithmetic: 19.1 us -> 4.11 us
  starting transfers between devices: 26 us -> 11.5 us
  between operations: 0.62 us -> 13.5 us
    all_to_all x3 -> x0, blocking collectives: 256 us -> none  [the longest x1 122 us: local(): lax.all_to_all(lax.all_to_all(outbound, 'ctx', split_axis=0, concat_axis=...]
    pallas_call x0 -> x2, Pallas kernels: none -> 223 us  [the longest x1 217 us: run_experts(): pl.pallas_call(expert_kernel, out_shape=jax.ShapeDtypeStruct((TOK, D), BF...]
    all_to_all x3 -> x0, waiting for transfers between devices: 134 us -> none  [the longest x1 119 us: local(): lax.all_to_all(lax.all_to_all(produced, 'ctx', split_axis=0, concat_axis=...]
    ppermute x2, waiting for transfers between devices: 120 us -> 0.01 us  [the longest x1 0.01 us: local(): other = lax.ppermute(routing, 'ctx', [(i, i ^ 1) for i in range(n_ctx)])]
    all_gather x0 -> x1, blocking collectives: none -> 83.3 us  [local(): routing = lax.all_gather(routing, 'exp', axis=0, tiled=True)]
    reshape x13 -> x3, local copies, waits for them, and re-layouts: 71.2 us -> 0.97 us  [the longest x1 0.87 us: local(): own_kv = own_kv.reshape(blocks, BLOCK_TOKENS, 2 * HEAD_SIZE)]
    dot_general x7 -> x1, matrix products: 31.4 us -> 0.36 us  [local(): rank = jnp.dot(member.astype(BF16), upper, preferred_element_type=F32)]
    all_to_all x5 -> x0, local copies, waits for them, and re-layouts: 24.4 us -> none  [the longest x1 7.93 us: local(): lax.all_to_all(lax.all_to_all(produced, 'ctx', split_axis=0, concat_axis=...]
  transfers between devices with their start and end apart: 5 -> 3, of which waited for: 4 -> 0; matrix products, arithmetic and copies ran while one was open for 2% -> 2% of each run, Pallas kernels for 0% -> 2%
where the time goes in v1:
time: 349 us; the launch traced here: 348 us
  Pallas kernels  223 us (64%)
  blocking collectives  83.3 us (24%)
  between operations  13.5 us (4%)
  local copies, waits for them, and re-layouts  12.5 us (4%)
  starting transfers between devices  11.5 us (3%)
  other arithmetic  4.11 us (1%)
    pallas_call x1, Pallas kernels, run_experts(): pl.pallas_call(expert_kernel, out_shape=jax.ShapeDtypeStruct((TOK, D), BF...  217 us
    all_gather x1, blocking collectives, local(): routing = lax.all_gather(routing, 'exp', axis=0, tiled=True)  83.3 us
    unnamed x14, local copies, waits for them, and re-layouts  7.89 us
  transfers between devices with their start and end apart: 3, of which 0 were waited for; matrix products, arithmetic and copies ran while one was open for 2% of the time, Pallas kernels for 2%

profile of v1, /device:TPU:1, one launch (start us, length us, event | category | flops | bytes accessed | tf_op | source)
XLA Modules:
  0.0 348.4 jit_solution(14405783212659985159)
XLA Ops:
  6.5 1.2 copy-done
  7.8 0.2 constant_dynamic-slice_fusion.2
  7.9 0.9 reshape.46
  8.8 4.9 %collective-permute-start.1 = (bf16[2048,1536]{1,0:T(8,128)(2,1)}, bf16[2048,1536]{1,0:T(8,128)(2,1)}, u32[]{:S(2)}, u32[]{:S(2)}) collective-permute-start(bf16[2048,1536]{1,0:T(8,128)(2,1)} %bitcast.24), channel_id=1, source_target_pairs={{1,8},{3,10},{5,12},{7,14},{8,1},{10,3},{12,5},{14,7},{17,24},{19,... | collective-permute-start | bytes 18874376 | tf_op jit(solution)/shard_map/ppermute | solution.py:521
  13.8 0.7 convert_element_type.41
  14.5 0.7 reduce_sum.18
  15.2 0.7 broadcast_divide_fusion
  15.9 83.3 %all-gather = f32[8,64,16]{1,2,0:T(8,128)S(1)} all-gather(f32[1,64,16]{1,2,0:T(8,128)S(1)} %maximum_bitcast_fusion), channel_id=1, replica_groups=mesh['ctx'=32,'exp'=8] {'exp'}, dimensions={0}, use_global_device_ids=true | all-gather | bytes 36864 | tf_op jit(solution)/shard_map/all_gather | solution.py:525
  99.3 6.5 %collective-permute-start = (f32[512,16]{0,1:T(8,128)S(1)}, f32[512,16]{0,1:T(8,128)S(1)}, u32[]{:S(2)}, u32[]{:S(2)}) collective-permute-start(f32[512,16]{0,1:T(8,128)S(1)} %reshape.51), channel_id=1, source_target_pairs={{0,8},{8,0},{16,24},{24,16},{32,40},{40,32},{48,56},{56,48},{64,72... | collective-permute-start | bytes 98312 | tf_op jit(solution)/shard_map/ppermute | solution.py:526
  105.8 0.8 constant_dynamic-slice_fusion.3
  106.7 0.7 constant_dynamic-slice_fusion.4
  107.8 0.2 and_reduce_fusion
  108.4 0.4 compare_reduce_fusion
  108.8 0.4 fusion.1
  109.2 0.4 fusion.2
  110.0 0.2 copy.47
  110.1 0.8 pad.7.pos_out
  110.9 0.8 pad.8.share_out
  111.7 0.7 dynamic-slice_convert_fusion.pos_in
  112.4 3.4 copy-done.1
  115.7 6.0 %attend.1.attn = bf16[512,512]{1,0:T(8,128)(2,1)S(1)} custom-call(s32[24]{0:T(128)S(1)} %max.8.ids, s32[24]{0:T(128)S(1)} %reshape.49.usable, bf16[512,512]{1,0:T(8,128)(2,1)S(1)} %copy-done.2, bf16[128,128,256]{2,1,0:T(8,128)(2,1)S(1)} %copy-done.1, bf16[128,128,256]{2,1,0:T(8,128)(2,1)S(1)} %copy-done.1, bf16[128,128,256]{2,1,0:T(8,128)(2,1)S(1)} %copy-done.1, ...), custom_call_target="tpu_custom_call" | custom-call | tf_op jit(solution)/shard_map/attend/pallas_call | solution.py:78
  121.8 0.8 copy-done.3
  122.6 217.1 %experts.1 = bf16[64,4096]{1,0:T(8,128)(2,1)} custom-call(bf16[512,512]{1,0:T(8,128)(2,1)} %copy-done.3, bf16[64,4096]{1,0:T(8,128)(2,1)} %resid.1, f32[1,4096]{1,0:T(1,128)} %bitcast.27, s32[16,1,1024]{2,1,0:T(1,128)} %dynamic-slice_convert_fusion.pos_in, bf16[1024,128]{1,0:T(8,128)(2,1)} %pad.7.pos_out, bf16[1024,128]{1,0:T(8,128)(2,1)} %pad.8.share_out, ...), custom_call_target="tpu_custom_call" | custom-call | flops 24999999488 | bytes 12000000 | tf_op jit(solution)/shard_map/experts/pallas_call | solution.py:457
  339.6 1.9 copy.49
  (32 shorter events, 1.4 us)
Async XLA Ops:
  6.5 1.2 copy-start
  6.5 105.8 %copy-start.2 = (bf16[512,512]{1,0:T(8,128)(2,1)S(1)}, bf16[512,512]{1,0:T(8,128)(2,1)}, u32[]{:S(2)}) copy-start(bf16[512,512]{1,0:T(8,128)(2,1)} %q_ref.1) | copy-start | bytes 1572868
  6.5 105.8 %all-gather.3.cloned.1.call-start = ((), (), s32[]{:S(2)}) async-start(), calls=%async_computation | async-start | bytes 8650752 | tf_op jit(solution)/shard_map/all_gather | solution.py:513
  8.8 113.7 %collective-permute-start.1 = (bf16[2048,1536]{1,0:T(8,128)(2,1)}, bf16[2048,1536]{1,0:T(8,128)(2,1)}, u32[]{:S(2)}, u32[]{:S(2)}) collective-permute-start(bf16[2048,1536]{1,0:T(8,128)(2,1)} %bitcast.24), channel_id=1, source_target_pairs={{1,8},{3,10},{5,12},{7,14},{8,1},{10,3},{12,5},{14,7},{17,24},{19,... | collective-permute-start | bytes 18874376 | tf_op jit(solution)/shard_map/ppermute | solution.py:521
  99.3 9.0 %collective-permute-start = (f32[512,16]{0,1:T(8,128)S(1)}, f32[512,16]{0,1:T(8,128)S(1)}, u32[]{:S(2)}, u32[]{:S(2)}) collective-permute-start(f32[512,16]{0,1:T(8,128)S(1)} %reshape.51), channel_id=1, source_target_pairs={{0,8},{8,0},{16,24},{24,16},{32,40},{40,32},{48,56},{56,48},{64,72... | collective-permute-start | bytes 98312 | tf_op jit(solution)/shard_map/ppermute | solution.py:526
  112.4 3.4 copy-start.1
  121.8 0.8 copy-start.3
Sparse Core Ops, SparseCore 0:
  9.9 62.1 all-gather.2

commit v2 on v1

v2 whole, which is shorter than its diff:
```python
import jax
import jax.numpy as jnp
from jax import lax
from jax.experimental import pallas as pl
from jax.experimental.pallas import tpu as pltpu
from jax.sharding import PartitionSpec as P

D = 4096
QUERY_HEADS = 32
KEY_VALUE_HEADS = 4
HEAD_SIZE = 128
FF = 768
TOPK = 8
BLOCK_TOKENS = 128
NV = 4
NS = 2
WINDOW = NS + NV

GRID = 4
CHIPS = GRID * GRID
PLANES = 8
TOK = 64
SPAN = PLANES * TOK
COLUMN = 2 * SPAN
CAP = 5
SLOTS = CAP * 2 * PLANES
GROUP = GRID * SLOTS
ROWS = CHIPS * SLOTS
HALF = D // 2
CHUNKS = 8
CHUNK = HALF // CHUNKS
HEADS = D // PLANES
EARLY = 896
LATE = (HALF - EARLY) // 2
MESH = pl.DeviceIdType.MESH
BF16 = jnp.bfloat16
F32 = jnp.float32


def attend_kernel(ids, usable, q_ref, *refs):
    kv, o_ref = refs[:WINDOW], refs[WINDOW]
    block = pl.program_id(0)
    heads = q_ref.shape[1] // HEAD_SIZE
    q = jnp.concatenate([q_ref[:, h * HEAD_SIZE : (h + 1) * HEAD_SIZE] for h in range(heads)], axis=0)
    keys = jnp.concatenate([kv[j][0, :, :HEAD_SIZE] for j in range(WINDOW)], axis=0)
    values = jnp.concatenate([kv[j][0, :, HEAD_SIZE:] for j in range(WINDOW)], axis=0)
    scores = lax.dot_general(q, keys, (((1,), (1,)), ((), ())), preferred_element_type=F32)
    scores = scores * HEAD_SIZE ** (-0.5)
    row = lax.broadcasted_iota(jnp.int32, (heads * BLOCK_TOKENS, BLOCK_TOKENS), 0) % BLOCK_TOKENS
    col = lax.broadcasted_iota(jnp.int32, (heads * BLOCK_TOKENS, BLOCK_TOKENS), 1)
    parts, masks = [], []
    for j in range(WINDOW):
        part = scores[:, j * BLOCK_TOKENS : (j + 1) * BLOCK_TOKENS]
        seen = jnp.full(part.shape, usable[block * WINDOW + j], jnp.int32) > 0
        if j == 0:
            seen = seen & (col <= row)
        parts.append(jnp.where(seen, part, -1e30))
        masks.append(seen)
    top = parts[0]
    for part in parts[1:]:
        top = jnp.maximum(top, part)
    top = jnp.max(top, axis=1, keepdims=True)
    parts = [jnp.where(seen, jnp.exp(part - top), 0.0) for part, seen in zip(parts, masks)]
    total = parts[0]
    for part in parts[1:]:
        total = total + part
    total = jnp.sum(total, axis=1, keepdims=True)
    probs = jnp.concatenate([(part / total).astype(BF16) for part in parts], axis=1)
    result = jnp.dot(probs, values, preferred_element_type=F32).astype(BF16)
    for h in range(heads):
        o_ref[:, h * HEAD_SIZE : (h + 1) * HEAD_SIZE] = result[h * BLOCK_TOKENS : (h + 1) * BLOCK_TOKENS]


def attend(queries, kv_blocks, ids, usable):
    blocks = queries.shape[0] // BLOCK_TOKENS
    width = queries.shape[1]

    def kv_spec(j):
        return pl.BlockSpec((1, BLOCK_TOKENS, 2 * HEAD_SIZE), lambda i, ids, usable: (ids[i * WINDOW + j], 0, 0))

    return pl.pallas_call(
        attend_kernel,
        grid_spec=pltpu.PrefetchScalarGridSpec(
            num_scalar_prefetch=2,
            grid=(blocks,),
            in_specs=[pl.BlockSpec((BLOCK_TOKENS, width), lambda i, ids, usable: (i, 0))]
            + [kv_spec(j) for j in range(WINDOW)],
            out_specs=pl.BlockSpec((BLOCK_TOKENS, width), lambda i, ids, usable: (i, 0)),
        ),
        out_shape=jax.ShapeDtypeStruct(queries.shape, BF16),
        compiler_params=pltpu.CompilerParams(vmem_limit_bytes=60 * 2**20),
        name="attend",
    )(ids, usable, queries, *([kv_blocks] * WINDOW))


def gather_kernel(own, w_own, kv, w_got, w_stage, s_s, s_r, b_s, b_r, o_s, x_s, x_r):
    ctx = lax.axis_index("ctx")
    z = lax.axis_index("exp")
    chip, c = lax.div(ctx, 2), lax.rem(ctx, 2)
    place = (lax.div(chip, GRID), lax.rem(chip, GRID))
    sibling = chip * 2 + 1 - c
    mate = lax.div(z, 2) * 2 + 1 - lax.rem(z, 2)
    same = c == lax.rem(z, 2)
    apart = c != lax.rem(z, 2)

    def chip_at(half, du, dv):
        u, v = place[half], place[1 - half]
        u, v = lax.rem(u + du + GRID, GRID), lax.rem(v + dv + GRID, GRID)
        return u * GRID + v if half == 0 else v * GRID + u

    def copy(src, dst, a_sem, b_sem, to_ctx, to_z):
        return pltpu.make_async_remote_copy(
            src_ref=src, dst_ref=dst, send_sem=a_sem, recv_sem=b_sem,
            device_id=(to_ctx, to_z), device_id_type=MESH,
        )

    barrier = pltpu.get_barrier_semaphore()

    def greet(cx, zz):
        pl.semaphore_signal(barrier, inc=1, device_id=(cx, zz), device_id_type=MESH)

    for half in range(2):
        for du in (1, -1):
            greet(chip_at(half, du, 0) * 2 + c, z)
    greet(sibling, z)
    greet(sibling, mate)
    greet(ctx, mate)
    pl.semaphore_wait(barrier, 7)

    first, second = pl.ds(0, EARLY // 2), pl.ds(EARLY // 2, EARLY // 2)

    def straight():
        return copy(w_own.at[first, :], w_got.at[first, :], x_s.at[0], x_r.at[0], sibling, mate)

    def to_stage():
        return copy(w_own.at[second, :], w_stage, x_s.at[1], x_r.at[1], sibling, z)

    def from_stage():
        return copy(w_stage, w_got.at[second, :], x_s.at[2], x_r.at[2], ctx, mate)

    @pl.when(apart)
    def _():
        to_stage().start()
        straight().start()

    started = []

    def launch(src, half, blocks, first, at, du, dv):
        to = chip_at(half, du, dv) * 2 + c
        dst = kv.at[at * 2 + c, pl.ds(first, blocks)]
        copy(src, dst, s_s.at[0], s_r.at[at, first], to, z).start()
        started.append(blocks)

    def held(at, first, blocks):
        return kv.at[at * 2 + c, pl.ds(first, blocks)]

    def arrive(at, first, blocks):
        ref = held(at, first, blocks)
        copy(ref, ref, s_s.at[0], s_r.at[at, first], ctx, z).wait_recv()

    def share(src, at, half):
        dst = kv.at[at * 2 + c, pl.ds(2 * half, 2)]
        copy(src, dst, b_s.at[0], b_r.at[0], sibling, z).start()

    for half in range(2):
        for du in (1, -1):
            launch(own.at[pl.ds(2 * half, 2)], half, 2, 2 * half, chip, du, 0)
    for half in range(2):
        for dv in (1, -1):
            launch(own.at[pl.ds(2 * half, 2)], half, 2, 2 * half, chip, 0, dv)
    for half in range(2):
        share(own.at[pl.ds(2 * half, 2)], chip, half)
    mine = pltpu.make_async_copy(own, kv.at[ctx], o_s.at[0])
    mine.start()

    def onward(half, du):
        at = chip_at(half, du, 0)
        for dv in (1, -1):
            launch(held(at, 2 * half, 2), half, 2, 2 * half, at, 0, dv)
        share(held(at, 2 * half, 2), at, half)

    for half in range(2):
        before, after = chip_at(half, -1, 0), chip_at(half, 1, 0)
        arrive(before, 2 * half, 2)
        launch(held(before, 2 * half, 1), half, 1, 2 * half, before, 1, 0)
        arrive(after, 2 * half, 2)
        launch(held(after, 2 * half + 1, 1), half, 1, 2 * half + 1, after, -1, 0)

    @pl.when(same)
    def _():
        to_stage().wait_recv()
        from_stage().start()

    for half in range(2):
        onward(half, -1)
        onward(half, 1)
    for half in range(2):
        far = chip_at(half, 2, 0)
        arrive(far, 2 * half, 1)
        arrive(far, 2 * half + 1, 1)
        onward(half, 2)
    for du in (0, -1, 1, 2):
        for half in range(2):
            before, after = chip_at(half, du, -1), chip_at(half, du, 1)
            arrive(before, 2 * half, 2)
            launch(held(before, 2 * half, 1), half, 1, 2 * half, before, 0, 1)
            arrive(after, 2 * half, 2)
            launch(held(after, 2 * half + 1, 1), half, 1, 2 * half + 1, after, 0, -1)
            share(held(before, 2 * half, 2), before, half)
            share(held(after, 2 * half, 2), after, half)
    for du in (0, -1, 1, 2):
        for half in range(2):
            far = chip_at(half, du, 2)
            arrive(far, 2 * half, 1)
            arrive(far, 2 * half + 1, 1)
            share(held(far, 2 * half, 2), far, half)

    def all_of(spans, s_sem, r_sem):
        return copy(kv.at[pl.ds(0, spans)], kv.at[pl.ds(0, spans)], s_sem.at[0], r_sem.at[0], sibling, z)

    all_of(CHIPS, b_s, b_r).wait_recv()
    all_of(CHIPS, b_s, b_r).wait_send()
    assert sum(started) % kv.shape[1] == 0
    all_of(sum(started) // kv.shape[1], s_s, b_r).wait_send()

    @pl.when(apart)
    def _():
        straight().wait()
        to_stage().wait_send()
        from_stage().wait_recv()

    @pl.when(same)
    def _():
        from_stage().wait_send()

    mine.wait()


def gather(own_kv, w_own):
    vmem = pl.BlockSpec(memory_space=pltpu.VMEM)
    hbm = pl.BlockSpec(memory_space=pl.ANY)
    dma = pltpu.SemaphoreType.DMA
    blocks = own_kv.shape[0]
    return pl.pallas_call(
        gather_kernel,
        out_shape=(
            jax.ShapeDtypeStruct((2 * CHIPS,) + own_kv.shape, BF16),
            jax.ShapeDtypeStruct((EARLY, 2 * FF), BF16),
            jax.ShapeDtypeStruct((EARLY // 2, 2 * FF), BF16),
        ),
        in_specs=[vmem, hbm],
        out_specs=(hbm, hbm, hbm),
        scratch_shapes=[
            dma((1,)), dma((CHIPS, blocks)),
            dma((1,)), dma((1,)),
            dma((1,)),
            dma((3,)), dma((3,)),
        ],
        compiler_params=pltpu.CompilerParams(collective_id=1, has_side_effects=True),
        cost_estimate=pl.CostEstimate(flops=0, bytes_accessed=100 * 10**6, transcendentals=0),
        name="gather",
    )(own_kv, w_own)


def expert_kernel(
    attn, resid, gain, route, w_own, w_got, w_out, out,
    routes, pos_in, pos_out, share_out, stage, heads_in, gath, toks, hot, sent, rows, win, wout, mine, theirs, hid_out, hid, back, comb, sib, parts,
    a_s, a_r, r_s, r_r, l_s, l_r, c_s, c_r, d_s, d_r, p_s, p_r, h_s, h_r, o_s, o_r, u_s, u_r, z_s, z_r, w_s, x_s, x_r, t_s, t_r,
):
    ctx = lax.axis_index("ctx")
    z = lax.axis_index("exp")
    chip, c = lax.div(ctx, 2), lax.rem(ctx, 2)
    x, y = lax.div(chip, GRID), lax.rem(chip, GRID)
    sibling = chip * 2 + 1 - c
    mate = lax.div(z, 2) * 2 + 1 - lax.rem(z, 2)
    same = c == lax.rem(z, 2)
    apart = c != lax.rem(z, 2)

    def send(src, dst, s_sem, r_sem, to_ctx, to_z):
        return pltpu.make_async_remote_copy(
            src_ref=src, dst_ref=dst, send_sem=s_sem, recv_sem=r_sem,
            device_id=(to_ctx, to_z), device_id_type=MESH,
        )

    def loop(count, body):
        lax.fori_loop(0, count, lambda i, carry: (body(i), carry)[1], 0)

    def mod8(v):
        return lax.rem(v + 2 * PLANES, PLANES)

    barrier = pltpu.get_barrier_semaphore()

    def greet(cx, zz):
        pl.semaphore_signal(barrier, inc=1, device_id=(cx, zz), device_id_type=MESH)

    def greet_chip(d):
        @pl.when(d != chip)
        def _():
            greet(d * 2 + c, z)

    loop(CHIPS, greet_chip)
    loop(PLANES - 1, lambda r: greet(ctx, mod8(z + r + 1)))
    greet(sibling, z)
    greet(sibling, mate)

    early, late = pl.ds(0, EARLY), pl.ds(EARLY, HALF - EARLY)
    straight, around = pl.ds(EARLY, LATE), pl.ds(EARLY + LATE, LATE)

    def win_copy(ref):
        return pltpu.make_async_copy(ref.at[early, :], win.at[early, :], w_s.at[0])

    def win_late():
        return pltpu.make_async_copy(w_own.at[late, :], win.at[late, :], w_s.at[1])

    def wout_copy(k):
        return pltpu.make_async_copy(w_out.at[:, pl.ds(k * CHUNK, CHUNK)], wout.at[k], w_s.at[2])

    def swap_late():
        return send(w_own.at[straight, :], win.at[straight, :], x_s.at[0], x_r.at[0], sibling, mate)

    def to_stage():
        return send(w_own.at[around, :], stage, x_s.at[1], x_r.at[1], sibling, z)

    def from_stage():
        return send(stage, win.at[around, :], x_s.at[2], x_r.at[2], ctx, mate)

    @pl.when(same)
    def _():
        win_copy(w_own).start()
        win_late().start()

    @pl.when(apart)
    def _():
        win_copy(w_got).start()

    for k in range(CHUNKS):
        wout_copy(k).start()

    def above(b):
        at = pl.ds(pl.multiple_of(b * 128, 128), 128)
        row = lax.broadcasted_iota(jnp.int32, (128, COLUMN), 0) + b * 128
        col = lax.broadcasted_iota(jnp.int32, (128, COLUMN), 1)
        mine[at, 0:COLUMN] = jnp.where(row < col, 1.0, 0.0).astype(BF16)

    loop(COLUMN // 128, above)
    pl.semaphore_wait(barrier, (CHIPS - 1) + (PLANES - 1) + 2)

    def a_send(r):
        to = mod8(z + r + 1)
        return send(attn.at[pl.ds(pl.multiple_of(to * TOK, TOK), TOK), :], heads_in.at[z], a_s.at[0], a_r.at[0], ctx, to)

    def tokens_of(core):
        return pl.ds(pl.multiple_of(core * SPAN, SPAN), SPAN)

    def place(core, slot):
        return pl.ds(pl.multiple_of(core * SPAN + slot * TOK, TOK), TOK)

    def t_send(r):
        to = mod8(z + r + 1)
        return send(route, routes.at[place(c, z), :], t_s.at[0], t_r.at[0], ctx, to)

    def t_across(core):
        at = tokens_of(core)
        return send(routes.at[at, :], routes.at[at, :], t_s.at[1], t_r.at[1], sibling, z)

    loop(PLANES - 1, lambda r: a_send(r).start())
    heads_in[z] = attn[pl.ds(pl.multiple_of(z * TOK, TOK), TOK), :]

    def a_all():
        ref = heads_in.at[pl.ds(0, PLANES - 1)]
        return send(ref, ref, a_s.at[0], a_r.at[0], ctx, z)

    a_all().wait_recv()

    squares = jnp.zeros((TOK, 1), F32)
    for b in range(PLANES):
        summed = resid[:, b * HEADS : (b + 1) * HEADS].astype(F32) + heads_in[b].astype(F32)
        squares = squares + jnp.sum(summed * summed, axis=1, keepdims=True)
    scale = lax.rsqrt(squares / D + 1e-06)

    def summed_at(b):
        at = slice(b * CHUNK, (b + 1) * CHUNK)
        plane, first = b * CHUNK // HEADS, b * CHUNK % HEADS
        return resid[:, at].astype(F32) + heads_in[plane, :, first : first + CHUNK].astype(F32)

    for b in range(2 * CHUNKS):
        normed = summed_at(b) * scale * gain[:, b * CHUNK : (b + 1) * CHUNK]
        gath[b % CHUNKS, z, b // CHUNKS] = normed.astype(BF16)

    def piece(k, r, slot, half):
        return gath.at[k, slot] if r < 4 else gath.at[k, slot, half]

    def right(k, r):
        ref = piece(k, r, mod8(z - r + 1), 0)
        return send(ref, ref, r_s.at[0], r_r.at[k, r - 1], ctx, mod8(z + 1))

    def left(k, r):
        ref = piece(k, r, mod8(z + r - 1), 1)
        return send(ref, ref, l_s.at[0], l_r.at[k, r - 1], ctx, mod8(z - 1))

    def right_in(k, r):
        ref = piece(k, r, mod8(z - r), 0)
        return send(ref, ref, r_s.at[0], r_r.at[k, r - 1], ctx, mod8(z + 1))

    def left_in(k, r):
        ref = piece(k, r, mod8(z + r), 1)
        return send(ref, ref, l_s.at[0], l_r.at[k, r - 1], ctx, mod8(z - 1))

    def across(k, slot):
        return send(
            gath.at[k, slot, 1 - c], toks.at[k, place(c, slot), :], c_s.at[0], c_r.at[k], sibling, z
        )

    def across_in(k):
        ref = toks.at[k, pl.ds(0, SPAN), :]
        return send(ref, ref, c_s.at[0], c_r.at[k], sibling, z)

    def arrived(k, slot):
        across(k, slot).start()
        toks[k, place(c, slot), :] = gath[k, slot, c]

    own = pl.ds(pl.multiple_of(chip * SLOTS, SLOTS), SLOTS)

    def d_send(k, d):
        at = pl.ds(pl.multiple_of(d * SLOTS, SLOTS), SLOTS)
        return send(sent.at[k, at, :], rows.at[own, pl.ds(k * CHUNK, CHUNK)], d_s.at[0], d_r.at[x], d * 2 + c, z)

    def dispatch(k):
        across_in(k).wait_recv()

        def step(g):
            xd = lax.rem(x + g, GRID)
            slot = lax.broadcasted_iota(jnp.int32, (SLOTS, COLUMN), 0)
            for i in range(GRID):
                hot[i * SLOTS : (i + 1) * SLOTS, :] = jnp.where(slot.astype(F32) == pos_in[xd * GRID + i], 1.0, 0.0).astype(BF16)
            at = pl.ds(pl.multiple_of(xd * GROUP, GROUP), GROUP)
            sent[k, at, :] = jnp.dot(hot[...], toks[k], preferred_element_type=F32).astype(BF16)
            for j in range(1, GRID):
                d_send(k, xd * GRID + lax.rem(y + j, GRID)).start()

            @pl.when(g > 0)
            def _():
                d_send(k, xd * GRID + y).start()

        loop(GRID, step)
        rows[own, k * CHUNK : (k + 1) * CHUNK] = sent[k, own, :]

    def lag(k):
        return k

    def t_all():
        ref = routes.at[pl.ds(0, (PLANES - 1) * TOK), :]
        return send(ref, ref, t_s.at[0], t_r.at[0], ctx, z)

    def ranks():
        table = jnp.transpose(routes[...])
        chips = lax.broadcasted_iota(jnp.int32, (CHIPS, COLUMN), 0) * PLANES + lax.div(z, 2)
        names_in = (chips + lax.rem(z, 2) * (PLANES // 2)).astype(F32)
        names_out = (chips + c * (PLANES // 2)).astype(F32)
        in_in, in_out = jnp.zeros((CHIPS, COLUMN), F32), jnp.zeros((CHIPS, COLUMN), F32)
        share = jnp.zeros((CHIPS, COLUMN), F32)
        for k in range(TOPK):
            named = table[k : k + 1]
            in_in = in_in + jnp.where(names_in == named, 1.0, 0.0)
            in_out = in_out + jnp.where(names_out == named, 1.0, 0.0)
            share = share + jnp.where(names_out == named, table[TOPK + k : TOPK + k + 1], 0.0)
        member = jnp.concatenate([in_in, in_out], axis=0)
        rank = jnp.dot(member.astype(BF16), mine[0:COLUMN, 0:COLUMN], preferred_element_type=F32)
        rank = jnp.where(member > 0.0, rank, -1.0)
        for d in range(CHIPS):
            pos_in[d] = rank[d : d + 1]
        blank = jnp.zeros((HEAD_SIZE - CHIPS, COLUMN), F32)
        pos_out[...] = jnp.transpose(jnp.concatenate([rank[CHIPS:], blank], axis=0)).astype(BF16)
        share_out[...] = jnp.transpose(jnp.concatenate([share, blank], axis=0)).astype(BF16)

    for tick in range(1, lag(CHUNKS - 1) + 6):
        for k in range(CHUNKS):
            r = tick - lag(k)
            if 2 <= r <= 5:
                right_in(k, r - 1).wait_recv()
                left_in(k, r - 1).wait_recv()
            if 1 <= r <= 4:
                right(k, r).start()
                left(k, r).start()
            if r == 1:
                arrived(k, z)
            if 2 <= r <= 4:
                arrived(k, mod8(z - r + 1))
                arrived(k, mod8(z + r - 1))
            if r == 5:
                arrived(k, mod8(z + 4))
        if tick == 1:
            loop(PLANES - 1, lambda r: t_send(r).start())
            routes[place(c, z), :] = route[...]

            @pl.when(apart)
            def _():
                to_stage().start()

        if tick == 2:
            t_all().wait_recv()
            t_across(c).start()
        if tick == 3:
            t_across(1 - c).wait_recv()
            ranks()
        for k in range(CHUNKS):
            if tick - lag(k) == 5:
                dispatch(k)
        if tick == CHUNKS + 3:

            @pl.when(apart)
            def _():
                swap_late().start()

            @pl.when(same)
            def _():
                to_stage().wait_recv()
                from_stage().start()

    lane = lax.broadcasted_iota(jnp.int32, (HEAD_SIZE, ROWS), 1)
    owner = lax.broadcasted_iota(jnp.int32, (HEAD_SIZE, ROWS), 0) * SLOTS
    spread = jnp.where((lane >= owner) & (lane < owner + SLOTS), 1.0, 0.0).astype(BF16)

    def build(b):
        at = pl.ds(pl.multiple_of(b * 128, 128), 128)
        slot = jnp.dot(pos_out[at, :], spread, preferred_element_type=F32)
        share = jnp.dot(share_out[at, :], spread, preferred_element_type=F32)
        want = lax.rem(lax.broadcasted_iota(jnp.int32, (128, ROWS), 1), SLOTS).astype(F32)
        comb[at, :] = jnp.where(slot == want, share, 0.0).astype(BF16)

    loop(COLUMN // 128, build)

    win_copy(w_own).wait()
    pltpu.make_async_copy(wout, wout, w_s.at[2]).wait()

    def span_of(g):
        xs = lax.rem(x - g + GRID, GRID)
        return xs, pl.ds(pl.multiple_of(xs * GROUP, GROUP), GROUP)

    def p_send(g):
        _, at = span_of(g)
        return send(mine.at[at, :], theirs.at[at, :], p_s.at[0], p_r.at[g], sibling, z)

    def first(g):
        xs, at = span_of(g)

        def from_row(count):
            ref = rows.at[pl.ds(0, count), :]
            send(ref, ref, d_s.at[0], d_r.at[xs], ctx, z).wait_recv()

        @pl.when(g == 0)
        def _():
            from_row(GROUP - SLOTS)

        @pl.when(g > 0)
        def _():
            from_row(GROUP)

        @pl.when((g == 0) & same)
        def _():
            win_late().wait()

        @pl.when((g == 0) & apart)
        def _():
            swap_late().wait_recv()
            from_stage().wait_recv()

        mine[at, :] = jnp.dot(rows[at, :], win[...], preferred_element_type=F32).astype(BF16)
        p_send(g).start()

    def h_send(g):
        at = pl.ds(pl.multiple_of(span_of(g)[0] * GROUP, GROUP), GROUP // 2)
        return send(hid_out.at[at, :], hid.at[at, :], h_s.at[0], h_r.at[g], sibling, mate)

    def h_same(g):
        at = pl.ds(pl.multiple_of(span_of(g)[0] * GROUP + GROUP // 2, GROUP // 2), GROUP // 2)
        return send(hid.at[at, :], hid.at[at, :], h_s.at[0], h_r.at[g], ctx, mate)

    def hidden(g):
        p_send(g).wait_recv()
        xs, _ = span_of(g)

        def part(i):
            at = pl.ds(pl.multiple_of(xs * GROUP + i * 32, 32), 32)
            pre = mine[at, :].astype(F32) + theirs[at, :].astype(F32)
            gate, up = pre[:, :FF], pre[:, FF:]
            value = (gate / (1.0 + jnp.exp(-gate)) * up).astype(BF16)

            @pl.when(same)
            def _():
                hid[at, :] = value

            @pl.when(apart)
            def _():
                hid_out[at, :] = value

        loop(GROUP // 32, part)

        @pl.when(apart)
        def _():
            h_send(g).start()

        @pl.when(same)
        def _():
            h_same(g).start()

    def first_and_hidden(g):
        @pl.when(g < GRID)
        def _():
            first(g)

        @pl.when(g > 0)
        def _():
            hidden(g - 1)

    loop(GRID + 1, first_and_hidden)

    def d_all(r_sem):
        ref = sent.at[:, pl.ds(0, ROWS - SLOTS), :]
        return send(ref, ref, d_s.at[0], r_sem, ctx, z)

    d_all(d_r.at[0]).wait_send()

    def o_send(n, d):
        at = pl.ds(pl.multiple_of(d * SLOTS, SLOTS), SLOTS)
        return send(sent.at[n, at, :], back.at[n, own, :], o_s.at[0], o_r.at[n], d * 2 + c, z)

    def second(n, g):
        xs, at = span_of(g)

        @pl.when((n == 0) & apart)
        def _():
            send(hid.at[at, :], hid.at[at, :], h_s.at[0], h_r.at[g], sibling, mate).wait_recv()

        sent[n, at, :] = jnp.dot(hid[at, :], wout[n], preferred_element_type=F32).astype(BF16)
        for j in range(1, GRID):
            o_send(n, xs * GRID + lax.rem(y + j, GRID)).start()

        @pl.when(g > 0)
        def _():
            o_send(n, xs * GRID + y).start()

        @pl.when(g == 0)
        def _():
            back[n, own, :] = sent[n, own, :]

    units = CHUNKS * 7 // 2 // 4
    for s_sem, r_sem in ((r_s, r_r), (l_s, l_r)):
        ref = gath.at[pl.ds(0, units), pl.ds(0, 4)]
        send(ref, ref, s_sem.at[0], r_sem.at[0, 0], ctx, z).wait_send()
    ref = gath.at[pl.ds(0, CHUNKS // 2)]
    send(ref, ref, c_s.at[0], c_r.at[0], ctx, z).wait_send()

    def u_send(n):
        return send(toks.at[n, pl.ds(0, SPAN), :], sib.at[n], u_s.at[0], u_r.at[n], sibling, z)

    def z_send(n, to):
        return send(gath.at[n, to, 0], parts.at[n, z], z_s.at[0], z_r.at[n], ctx, to)

    def combine(step):
        @pl.when(step < CHUNKS)
        def _():
            loop(GRID, lambda g: second(step, g))

        @pl.when(step > 1)
        def _():
            n = step - 2

            ref = back.at[n, pl.ds(0, ROWS - SLOTS), :]
            send(ref, ref, o_s.at[0], o_r.at[n], ctx, z).wait_recv()
            toks[n, pl.ds(0, SPAN), :] = jnp.dot(
                comb[tokens_of(1 - c), :], back[n], preferred_element_type=F32
            ).astype(BF16)
            u_send(n).start()
            total = jnp.dot(comb[tokens_of(c), :], back[n], preferred_element_type=F32)
            u_send(n).wait_recv()
            total = (total + sib[n].astype(F32)).astype(BF16)
            for s in range(PLANES):
                gath[n, s, 0] = total[s * TOK : (s + 1) * TOK]
            loop(PLANES - 1, lambda r: z_send(n, mod8(z + r + 1)).start())
            parts[n, z] = gath[n, z, 0]

    loop(CHUNKS + 2, combine)

    for n in range(CHUNKS):
        ref = parts.at[n, pl.ds(0, PLANES - 1)]
        send(ref, ref, z_s.at[0], z_r.at[n], ctx, z).wait_recv()
        for half in range(2):
            b = half * CHUNKS + n
            total = parts[n, half].astype(F32)
            for q in range(1, PLANES // 2):
                total = total + parts[n, 2 * q + half].astype(F32)
            out[:, b * CHUNK : (b + 1) * CHUNK] = (summed_at(b) + total).astype(BF16)

    a_all().wait_send()
    send(mine, mine, p_s.at[0], p_r.at[0], ctx, z).wait_send()
    ref = hid.at[pl.ds(0, ROWS // 2), :]
    send(ref, ref, h_s.at[0], h_r.at[0], ctx, z).wait_send()
    ref = sent.at[:, pl.ds(0, ROWS - SLOTS), :]
    send(ref, ref, o_s.at[0], o_r.at[0], ctx, z).wait_send()
    ref = toks.at[:, pl.ds(0, SPAN), :]
    send(ref, ref, u_s.at[0], u_r.at[0], ctx, z).wait_send()
    ref = parts.at[:, pl.ds(0, PLANES - 1)]
    send(ref, ref, z_s.at[0], z_r.at[0], ctx, z).wait_send()

    @pl.when(apart)
    def _():
        swap_late().wait_send()
        to_stage().wait_send()

    @pl.when(same)
    def _():
        from_stage().wait_send()

    t_all().wait_send()
    t_across(c).wait_send()


def run_experts(attn, resid, gain, route, w_own, w_got, w_out):
    vmem = pl.BlockSpec(memory_space=pltpu.VMEM)
    hbm = pl.BlockSpec(memory_space=pl.ANY)
    dma = pltpu.SemaphoreType.DMA
    return pl.pallas_call(
        expert_kernel,
        out_shape=jax.ShapeDtypeStruct((TOK, D), BF16),
        in_specs=[vmem] * 4 + [hbm] * 3,
        out_specs=vmem,
        scratch_shapes=[
            pltpu.VMEM((COLUMN, HEAD_SIZE), F32),
            pltpu.VMEM((CHIPS, 1, COLUMN), F32),
            pltpu.VMEM((COLUMN, HEAD_SIZE), BF16),
            pltpu.VMEM((COLUMN, HEAD_SIZE), BF16),
            pltpu.VMEM((LATE, 2 * FF), BF16),
            pltpu.VMEM((PLANES, TOK, HEADS), BF16),
            pltpu.VMEM((CHUNKS, PLANES, 2, TOK, CHUNK), BF16),
            pltpu.VMEM((CHUNKS, COLUMN, CHUNK), BF16),
            pltpu.VMEM((GROUP, COLUMN), BF16),
            pltpu.VMEM((CHUNKS, ROWS, CHUNK), BF16),
            pltpu.VMEM((ROWS, HALF), BF16),
            pltpu.VMEM((HALF, 2 * FF), BF16),
            pltpu.VMEM((CHUNKS, FF, CHUNK), BF16),
            pltpu.VMEM((ROWS, 2 * FF), BF16),
            pltpu.VMEM((ROWS, 2 * FF), BF16),
            pltpu.VMEM((ROWS, FF), BF16),
            pltpu.VMEM((ROWS, FF), BF16),
            pltpu.VMEM((CHUNKS, ROWS, CHUNK), BF16),
            pltpu.VMEM((COLUMN, ROWS), BF16),
            pltpu.VMEM((CHUNKS, SPAN, CHUNK), BF16),
            pltpu.VMEM((CHUNKS, PLANES, TOK, CHUNK), BF16),
            dma((1,)), dma((1,)),
            dma((1,)), dma((CHUNKS, 4)),
            dma((1,)), dma((CHUNKS, 4)),
            dma((1,)), dma((CHUNKS,)),
            dma((1,)), dma((GRID,)),
            dma((1,)), dma((GRID,)),
            dma((1,)), dma((GRID,)),
            dma((1,)), dma((CHUNKS,)),
            dma((1,)), dma((CHUNKS,)),
            dma((1,)), dma((CHUNKS,)),
            dma((3,)),
            dma((3,)), dma((3,)),
            dma((2,)), dma((2,)),
        ],
        compiler_params=pltpu.CompilerParams(
            collective_id=0, has_side_effects=True, vmem_limit_bytes=62 * 2**20
        ),
        cost_estimate=pl.CostEstimate(flops=25 * 10**9, bytes_accessed=12 * 10**6, transcendentals=10**6),
        name="experts",
    )(attn, resid, gain, route, w_own, w_got, w_out)


def local(
    queries, key_value_stack, vertical_cols, slash_offsets, resid,
    norm_gain, expert_ids, gate_weights, w_in, w_out,
):
    ctx = lax.axis_index("ctx")
    z = lax.axis_index("exp")
    blocks = queries.shape[0] // BLOCK_TOKENS
    heads_dev = queries.shape[1] // HEAD_SIZE

    kv_head = z * heads_dev // (QUERY_HEADS // KEY_VALUE_HEADS)
    own_kv = lax.dynamic_slice_in_dim(key_value_stack, kv_head * HEAD_SIZE, HEAD_SIZE, 2)
    own_kv = own_kv.reshape(blocks, BLOCK_TOKENS, 2 * HEAD_SIZE)

    w_own = w_in[0]

    shares = gate_weights / jnp.sum(gate_weights, axis=1, keepdims=True)
    routing = jnp.concatenate([expert_ids.astype(F32), shares], axis=1)
    routing = jnp.pad(routing, ((0, 0), (0, HEAD_SIZE - 2 * TOPK)))
    kv, w_got, _ = gather(own_kv, w_own)
    kv_blocks = kv.reshape(-1, BLOCK_TOKENS, 2 * HEAD_SIZE)

    first = ctx * blocks
    cols = lax.dynamic_slice_in_dim(vertical_cols, first, blocks, 0)
    offsets = lax.dynamic_slice_in_dim(slash_offsets, first, blocks, 0)
    slash = (first + jnp.arange(blocks, dtype=jnp.int32))[:, None] - offsets
    in_slash = jnp.any(cols[:, :, None] == slash[:, None, :], axis=2)
    earlier = jnp.arange(NV)[None, :] < jnp.arange(NV)[:, None]
    repeated = jnp.any((cols[:, :, None] == cols[:, None, :]) & earlier[None], axis=2)
    usable = jnp.concatenate([slash >= 0, (cols >= 0) & ~in_slash & ~repeated], axis=1)
    chosen = jnp.maximum(jnp.concatenate([slash, cols], axis=1), 0)
    attn = attend(queries, kv_blocks, chosen.reshape(-1), usable.astype(jnp.int32).reshape(-1))

    return run_experts(attn, resid, norm_gain[None, :], routing, w_own, w_got, w_out[0])


def solution(mesh):
    in_specs = (
        P("ctx", "exp"),
        P("ctx", None, None),
        P(),
        P(),
        P(("ctx", "exp"), None),
        P(),
        P(("ctx", "exp"), None),
        P(("ctx", "exp"), None),
        P(("ctx", "exp"), None, None),
        P(("ctx", "exp"), None, None),
    )
    out_specs = P(("ctx", "exp"), None)
    return jax.shard_map(local, mesh=mesh, in_specs=in_specs, out_specs=out_specs, check_vma=False)
```

time: 349 us -> 267 us (0.77)
  blocking collectives: 83.3 us -> 0 us
  Pallas kernels: 223 us -> 259 us
  between operations: 13.5 us -> 0.07 us
  starting transfers between devices: 11.5 us -> 0 us
  local copies, waits for them, and re-layouts: 12.5 us -> 6.58 us
  other arithmetic: 4.11 us -> 0.59 us
    all_gather x1 -> x0, blocking collectives: 83.3 us -> none  [local(): routing = lax.all_gather(routing, 'exp', axis=0, tiled=True)]
    pallas_call x0 -> x1, Pallas kernels: none -> 38.7 us  [gather(): pl.pallas_call(gather_kernel, out_shape=(jax.ShapeDtypeStruct((2 * CHIPS,...]
    ppermute x2 -> x0, starting transfers between devices: 11.5 us -> none  [the longest x1 6.51 us: local(): other = lax.ppermute(routing, 'ctx', [(i, i ^ 1) for i in range(n_ctx)])]
    pallas_call x1, Pallas kernels: 217 us -> 212 us  [run_experts(): pl.pallas_call(expert_kernel, out_shape=jax.ShapeDtypeStruct((TOK, D), BF...]
    unnamed x14 -> x13, local copies, waits for them, and re-layouts: 7.89 us -> 3.3 us
  transfers between devices with their start and end apart: 3 -> 0, of which waited for: 0 -> 0; matrix products, arithmetic and copies ran while one was open for 2% -> 0% of each run, Pallas kernels for 2% -> 0%
where the time goes in v2:
time: 267 us
  Pallas kernels  259 us (97%)
  local copies, waits for them, and re-layouts  6.58 us (2%)
    pallas_call x1, Pallas kernels, run_experts(): pl.pallas_call(expert_kernel, out_shape=jax.ShapeDtypeStruct((TOK, D), BF...  212 us
    pallas_call x1, Pallas kernels, gather(): pl.pallas_call(gather_kernel, out_shape=(jax.ShapeDtypeStruct((2 * CHIPS,...  38.7 us
    pallas_call x1, Pallas kernels, attend(): pl.pallas_call(attend_kernel, grid_spec=pltpu.PrefetchScalarGridSpec(num_...  8.34 us

profile of v2, /device:TPU:1, one launch (start us, length us, event | category | flops | bytes accessed | tf_op | source)
XLA Modules:
  0.0 266.7 jit_solution(15654534602070015176)
XLA Ops:
  0.0 0.0 copy-start
  0.0 1.2 copy-done
  1.2 0.2 constant_dynamic-slice_fusion
  1.4 0.9 reshape.34.own
  2.3 38.7 %gather.1 = (bf16[32,4,128,256]{3,2,1,0:T(8,128)(2,1)}, bf16[896,1536]{1,0:T(8,128)(2,1)}, bf16[448,1536]{1,0:T(8,128)(2,1)}) custom-call(bf16[4,128,256]{2,1,0:T(8,128)(2,1)} %reshape.34.own, bf16[2048,1536]{1,0:T(8,128)(2,1)} %bitcast.10), custom_call_target="tpu_custom_call" | custom-call | bytes 100000000 | tf_op jit(solution)/shard_map/gather/pallas_call | solution.py:244
  41.0 0.0 copy-done.4
  41.0 0.1 constant_dynamic-slice_fusion.2
  41.1 0.1 copy.31
  41.2 0.1 broadcast_compare_fusion
  41.3 0.1 copy.29
  41.4 0.0 copy-done.3
  41.4 0.1 constant_dynamic-slice_fusion.1
  41.5 0.1 copy.32
  41.6 0.1 compare_reduce_fusion
  41.7 0.2 and_reduce_fusion
  41.9 0.1 add_convert_fusion
  42.0 0.7 reshape.36.usable
  42.6 0.1 add_maximum_fusion
  42.7 0.6 max.8.ids
  43.3 8.3 %attend.1.attn = bf16[512,512]{1,0:T(8,128)(2,1)} custom-call(s32[24]{0:T(128)} %max.8.ids, s32[24]{0:T(128)} %reshape.36.usable, bf16[512,512]{1,0:T(8,128)(2,1)} %q_ref.1, bf16[128,128,256]{2,1,0:T(8,128)(2,1)} %bitcast.4, bf16[128,128,256]{2,1,0:T(8,128)(2,1)} %bitcast.5, bf16[128,128,256]{2,1,0:T(8,128)(2,1)} %bitcast.6, bf16[128,128,256]{2,1,0:T(8,128)(2,1)} %bitcast.7, ...), custom_call_target="tpu_custom_call" | custom-call | tf_op jit(solution)/shard_map/attend/pallas_call | solution.py:81
  51.7 0.1 copy.30
  51.8 0.6 pad.4.route
  52.4 212.4 %experts.1 = bf16[64,4096]{1,0:T(8,128)(2,1)} custom-call(bf16[512,512]{1,0:T(8,128)(2,1)} %attend.1.attn, bf16[64,4096]{1,0:T(8,128)(2,1)} %resid.1, f32[1,4096]{1,0:T(1,128)} %bitcast.13, f32[64,128]{1,0:T(8,128)} %pad.4.route, bf16[2048,1536]{1,0:T(8,128)(2,1)} %bitcast.11, bf16[896,1536]{1,0:T(8,128)(2,1)} %get-tuple-element.8.w_got, ...), custom_call_target="tpu_custom_call" | custom-call | flops 24999999488 | bytes 12000000 | tf_op jit(solution)/shard_map/experts/pallas_call | solution.py:723
  264.8 1.9 copy.34
  (13 shorter events, 0.1 us)
Async XLA Ops:
  0.0 1.2 copy-start
  2.3 38.8 %copy-start.4 = (s32[128,2]{0,1:T(2,128)S(1)}, s32[128,2]{0,1:T(2,128)}, u32[]{:S(2)}) copy-start(s32[128,2]{0,1:T(2,128)} %param.13) | copy-start | bytes 3076
  2.3 39.1 %copy-start.3 = (s32[128,4]{0,1:T(4,128)S(1)}, s32[128,4]{0,1:T(4,128)}, u32[]{:S(2)}) copy-start(s32[128,4]{0,1:T(4,128)} %param.12) | copy-start | bytes 6148
  43.3 8.3 %copy-start.1 = (f32[64,8]{0,1:T(8,128)S(1)}, f32[64,8]{0,1:T(8,128)}, u32[]{:S(2)}) copy-start(f32[64,8]{0,1:T(8,128)} %param.17) | copy-start | bytes 6148
  43.3 8.4 %copy-start.2 = (s32[64,8]{0,1:T(8,128)S(1)}, s32[64,8]{0,1:T(8,128)}, u32[]{:S(2)}) copy-start(s32[64,8]{0,1:T(8,128)} %param.16) | copy-start | bytes 6148

commit v3 on v1

v3 whole, which is shorter than its diff:
```python
import jax
import jax.numpy as jnp
from jax import lax
from jax.experimental import pallas as pl
from jax.experimental.pallas import tpu as pltpu
from jax.sharding import PartitionSpec as P

D = 4096
QUERY_HEADS = 32
KEY_VALUE_HEADS = 4
HEAD_SIZE = 128
FF = 768
TOPK = 8
BLOCK_TOKENS = 128
NV = 4
NS = 2
WINDOW = NS + NV

GRID = 4
CHIPS = GRID * GRID
PLANES = 8
TOK = 64
SPAN = PLANES * TOK
COLUMN = 2 * SPAN
CAP = 5
SLOTS = CAP * 2 * PLANES
GROUP = GRID * SLOTS
ROWS = CHIPS * SLOTS
HALF = D // 2
CHUNKS = 8
CHUNK = HALF // CHUNKS
HEADS = D // PLANES
PIECES = 16
PIECE = HALF // 2 // PIECES
EARLY = 5
RING = (5, 6, 7, 8, 9, 10, 11)
LAPS = tuple((k, 1) for k in range(CHUNKS))
VMEM_BYTES = 63 * 2**20
MESH = pl.DeviceIdType.MESH
BF16 = jnp.bfloat16
F32 = jnp.float32


def attend(q, kv, seen_blocks):
    heads = q.shape[1] // HEAD_SIZE
    q = jnp.concatenate([q[:, h * HEAD_SIZE : (h + 1) * HEAD_SIZE] for h in range(heads)], axis=0)
    keys = jnp.concatenate([block[:, :HEAD_SIZE] for block in kv], axis=0)
    values = jnp.concatenate([block[:, HEAD_SIZE:] for block in kv], axis=0)
    scores = lax.dot_general(q, keys, (((1,), (1,)), ((), ())), preferred_element_type=F32)
    scores = scores * HEAD_SIZE ** (-0.5)
    row = lax.broadcasted_iota(jnp.int32, (heads * BLOCK_TOKENS, BLOCK_TOKENS), 0) % BLOCK_TOKENS
    col = lax.broadcasted_iota(jnp.int32, (heads * BLOCK_TOKENS, BLOCK_TOKENS), 1)
    parts, masks = [], []
    for j in range(WINDOW):
        part = scores[:, j * BLOCK_TOKENS : (j + 1) * BLOCK_TOKENS]
        seen = jnp.full(part.shape, seen_blocks[j], jnp.int32) > 0
        if j == 0:
            seen = seen & (col <= row)
        parts.append(jnp.where(seen, part, -1e30))
        masks.append(seen)
    top = parts[0]
    for part in parts[1:]:
        top = jnp.maximum(top, part)
    top = jnp.max(top, axis=1, keepdims=True)
    parts = [jnp.where(seen, jnp.exp(part - top), 0.0) for part, seen in zip(parts, masks)]
    total = parts[0]
    for part in parts[1:]:
        total = total + part
    total = jnp.sum(total, axis=1, keepdims=True)
    probs = jnp.concatenate([(part / total).astype(BF16) for part in parts], axis=1)
    result = jnp.dot(probs, values, preferred_element_type=F32).astype(BF16)
    return jnp.concatenate([result[h * BLOCK_TOKENS : (h + 1) * BLOCK_TOKENS] for h in range(heads)], axis=1)


def layer_kernel(
    cols, offsets, own, queries, ids, gates, resid, gain, w_own, w_out, out, w_stage,
    kv, route, routes, pos_in, pos_out, share_out, heads_in, gath, toks, hot, rows, win, wout,
    mine, theirs, hid_out, hid, back, comb, sib, parts,
    s_s, s_r, b_s, b_r, o_c, a_s, a_r, t_s, t_r,
    r_s, r_r, l_s, l_r, c_s, c_r, d_s, d_r, p_s, p_r, h_s, h_r, o_s, o_r, u_s, u_r, z_s, z_r, w_s, x_s, x_r,
):
    ctx = lax.axis_index("ctx")
    z = lax.axis_index("exp")
    chip, c = lax.div(ctx, 2), lax.rem(ctx, 2)
    x, y = lax.div(chip, GRID), lax.rem(chip, GRID)
    sibling = chip * 2 + 1 - c
    mate = lax.div(z, 2) * 2 + 1 - lax.rem(z, 2)
    same = c == lax.rem(z, 2)
    apart = c != lax.rem(z, 2)

    def send(src, dst, s_sem, r_sem, to_ctx, to_z):
        return pltpu.make_async_remote_copy(
            src_ref=src, dst_ref=dst, send_sem=s_sem, recv_sem=r_sem,
            device_id=(to_ctx, to_z), device_id_type=MESH,
        )

    def loop(count, body):
        lax.fori_loop(0, count, lambda i, carry: (body(i), carry)[1], 0)

    def mod8(v):
        return lax.rem(v + 2 * PLANES, PLANES)

    barrier = pltpu.get_barrier_semaphore()

    def greet(cx, zz):
        pl.semaphore_signal(barrier, inc=1, device_id=(cx, zz), device_id_type=MESH)

    def greet_chip(d):
        @pl.when(d != chip)
        def _():
            greet(d * 2 + c, z)

    loop(CHIPS, greet_chip)
    loop(PLANES - 1, lambda r: greet(ctx, mod8(z + r + 1)))
    greet(sibling, z)
    greet(sibling, mate)

    def wout_copy(k):
        return pltpu.make_async_copy(w_out.at[:, pl.ds(k * CHUNK, CHUNK)], wout.at[k], w_s.at[1])

    def piece_rows(first, p):
        return pl.ds(pl.multiple_of(first + p * PIECE, PIECE), PIECE)

    def straight(p):
        at = piece_rows(0, p)
        return send(w_own.at[at, :], win.at[at, :], x_s.at[0], x_r.at[0], sibling, mate)

    def to_stage():
        return send(w_own.at[pl.ds(HALF // 2, HALF // 2), :], w_stage, x_s.at[1], x_r.at[1], sibling, z)

    def from_stage(p):
        src, dst = piece_rows(0, p), piece_rows(HALF // 2, p)
        return send(w_stage.at[src, :], win.at[dst, :], x_s.at[2], x_r.at[2], ctx, mate)

    def next_piece(p):
        @pl.when(apart)
        def _():
            straight(p).start()

        @pl.when(same)
        def _():
            from_stage(p).start()

    @pl.when(same)
    def _():
        pltpu.make_async_copy(w_own, win, w_s.at[0]).start()

    for k in range(CHUNKS):
        wout_copy(k).start()

    def above(b):
        at = pl.ds(pl.multiple_of(b * 128, 128), 128)
        row = lax.broadcasted_iota(jnp.int32, (128, COLUMN), 0) + b * 128
        col = lax.broadcasted_iota(jnp.int32, (128, COLUMN), 1)
        mine[at, 0:COLUMN] = jnp.where(row < col, 1.0, 0.0).astype(BF16)

    loop(COLUMN // 128, above)

    def tokens_of(core):
        return pl.ds(pl.multiple_of(core * SPAN, SPAN), SPAN)

    def place(core, slot):
        return pl.ds(pl.multiple_of(core * SPAN + slot * TOK, TOK), TOK)

    shares = gates[...] / jnp.sum(gates[...], axis=0, keepdims=True)
    blank = jnp.zeros((HEAD_SIZE - 2 * TOPK, TOK), F32)
    both = jnp.concatenate([ids[...].astype(F32), shares, blank], axis=0)
    both = jnp.concatenate([both, jnp.zeros((HEAD_SIZE, HEAD_SIZE - TOK), F32)], axis=1)
    route[...] = jnp.transpose(both)[:TOK]
    routes[place(c, z), :] = route[...]

    def t_send(to):
        return send(route, routes.at[place(c, z), :], t_s.at[0], t_r.at[0], ctx, to)

    def t_all():
        ref = routes.at[pl.ds(0, (PLANES - 1) * TOK), :]
        return send(ref, ref, t_s.at[0], t_r.at[0], ctx, z)

    def t_across(core):
        at = tokens_of(core)
        return send(routes.at[at, :], routes.at[at, :], t_s.at[1], t_r.at[1], sibling, z)

    spot = (x, y)

    def chip_at(half, du, dv):
        u, v = spot[half], spot[1 - half]
        u, v = lax.rem(u + du + GRID, GRID), lax.rem(v + dv + GRID, GRID)
        return u * GRID + v if half == 0 else v * GRID + u

    pl.semaphore_wait(barrier, (CHIPS - 1) + (PLANES - 1) + 2)

    per = SPAN // BLOCK_TOKENS
    started = []

    def blocks_at(first, count):
        return kv.at[pl.ds(first, count)]

    def own_at(first, count):
        return own.at[pl.ds(first, count)]

    def launch(src, half, blocks, first, at, du, dv):
        to = chip_at(half, du, dv) * 2 + c
        dst = blocks_at((at * 2 + c) * per + first, blocks)
        send(src, dst, s_s.at[0], s_r.at[at, first], to, z).start()
        started.append(blocks)

    def held(at, first, blocks):
        return blocks_at((at * 2 + c) * per + first, blocks)

    def arrive(at, first, blocks):
        ref = held(at, first, blocks)
        send(ref, ref, s_s.at[0], s_r.at[at, first], ctx, z).wait_recv()

    def share(src, at, half):
        dst = blocks_at((at * 2 + c) * per + 2 * half, 2)
        send(src, dst, b_s.at[0], b_r.at[0], sibling, z).start()

    for half in range(2):
        for du in (1, -1):
            launch(own_at(2 * half, 2), half, 2, 2 * half, chip, du, 0)
    for half in range(2):
        for dv in (1, -1):
            launch(own_at(2 * half, 2), half, 2, 2 * half, chip, 0, dv)
    for half in range(2):
        share(own_at(2 * half, 2), chip, half)
    own_copy = pltpu.make_async_copy(own, blocks_at(ctx * per, per), o_c.at[0])
    own_copy.start()
    loop(PLANES - 1, lambda r: t_send(mod8(z + r + 1)).start())

    @pl.when(apart)
    def _():
        to_stage().start()
        loop(EARLY, lambda p: straight(p).start())

    def onward(half, du):
        at = chip_at(half, du, 0)
        for dv in (1, -1):
            launch(held(at, 2 * half, 2), half, 2, 2 * half, at, 0, dv)
        share(held(at, 2 * half, 2), at, half)

    for half in range(2):
        before, after = chip_at(half, -1, 0), chip_at(half, 1, 0)
        arrive(before, 2 * half, 2)
        launch(held(before, 2 * half, 1), half, 1, 2 * half, before, 1, 0)
        arrive(after, 2 * half, 2)
        launch(held(after, 2 * half + 1, 1), half, 1, 2 * half + 1, after, -1, 0)

    @pl.when(same)
    def _():
        to_stage().wait_recv()
        loop(EARLY, lambda p: from_stage(p).start())

    for half in range(2):
        onward(half, -1)
        onward(half, 1)
    t_all().wait_recv()
    t_across(c).start()
    for half in range(2):
        far = chip_at(half, 2, 0)
        arrive(far, 2 * half, 1)
        arrive(far, 2 * half + 1, 1)
        onward(half, 2)
    for du in (0, -1, 1, 2):
        for half in range(2):
            before, after = chip_at(half, du, -1), chip_at(half, du, 1)
            arrive(before, 2 * half, 2)
            launch(held(before, 2 * half, 1), half, 1, 2 * half, before, 0, 1)
            arrive(after, 2 * half, 2)
            launch(held(after, 2 * half + 1, 1), half, 1, 2 * half + 1, after, 0, -1)
            share(held(before, 2 * half, 2), before, half)
            share(held(after, 2 * half, 2), after, half)
    for du in (0, -1, 1, 2):
        for half in range(2):
            far = chip_at(half, du, 2)
            arrive(far, 2 * half, 1)
            arrive(far, 2 * half + 1, 1)
            share(held(far, 2 * half, 2), far, half)

    def all_of(blocks, s_sem, r_sem):
        ref = blocks_at(0, blocks)
        return send(ref, ref, s_sem.at[0], r_sem.at[0], sibling, z)

    all_of(CHIPS * per, b_s, b_r).wait_recv()
    own_copy.wait()

    def a_send(to):
        at = pl.ds(pl.multiple_of(to * TOK, TOK), TOK)
        return send(comb.at[at, pl.ds(0, HEADS)], heads_in.at[z], a_s.at[0], a_r.at[0], ctx, to)

    def block(turn, carry):
        i = lax.rem(turn + lax.div(z, 2) + 1, SPAN // BLOCK_TOKENS)
        at = pl.ds(pl.multiple_of(i * BLOCK_TOKENS, BLOCK_TOKENS), BLOCK_TOKENS)
        number = ctx * per + i
        slash = [number - offsets[j, number] for j in range(NS)]
        column = [cols[j, number] for j in range(NV)]
        kept = [v >= 0 for v in slash]
        for j in range(NV):
            keep = column[j] >= 0
            for other in slash + column[:j]:
                keep = jnp.logical_and(keep, column[j] != other)
            kept.append(keep)
        chosen = [kv[jnp.maximum(v, 0)] for v in slash + column]
        kept = [jnp.where(v, 1, 0) for v in kept]
        comb[at, 0:HEADS] = attend(queries[at, :], chosen, kept)
        for part in range(BLOCK_TOKENS // TOK):
            to = i * (BLOCK_TOKENS // TOK) + part

            @pl.when(to != z)
            def _():
                a_send(to).start()

        return carry

    lax.fori_loop(0, SPAN // BLOCK_TOKENS, block, 0)
    heads_in[z] = comb[pl.ds(pl.multiple_of(z * TOK, TOK), TOK), 0:HEADS]

    t_across(1 - c).wait_recv()
    table = jnp.transpose(routes[...])
    chips = lax.broadcasted_iota(jnp.int32, (CHIPS, COLUMN), 0) * PLANES + lax.div(z, 2)
    names_in = (chips + lax.rem(z, 2) * (PLANES // 2)).astype(F32)
    names_out = (chips + c * (PLANES // 2)).astype(F32)
    in_in, in_out = jnp.zeros((CHIPS, COLUMN), F32), jnp.zeros((CHIPS, COLUMN), F32)
    weight = jnp.zeros((CHIPS, COLUMN), F32)
    for k in range(TOPK):
        named = table[k : k + 1]
        in_in = in_in + jnp.where(names_in == named, 1.0, 0.0)
        in_out = in_out + jnp.where(names_out == named, 1.0, 0.0)
        weight = weight + jnp.where(names_out == named, table[TOPK + k : TOPK + k + 1], 0.0)
    member = jnp.concatenate([in_in, in_out], axis=0)
    rank = jnp.dot(member.astype(BF16), mine[0:COLUMN, 0:COLUMN], preferred_element_type=F32)
    rank = jnp.where(member > 0.0, rank, -1.0)
    for d in range(CHIPS):
        pos_in[d] = rank[d : d + 1]
    blank = jnp.zeros((HEAD_SIZE - CHIPS, COLUMN), F32)
    pos_out[...] = jnp.transpose(jnp.concatenate([rank[CHIPS:], blank], axis=0)).astype(BF16)
    share_out[...] = jnp.transpose(jnp.concatenate([weight, blank], axis=0)).astype(BF16)

    ref = heads_in.at[pl.ds(0, PLANES - 1)]
    send(ref, ref, a_s.at[0], a_r.at[0], ctx, z).wait()
    all_of(CHIPS * per, b_s, b_r).wait_send()
    all_of(sum(started), s_s, b_r).wait_send()
    t_all().wait_send()
    t_across(c).wait_send()

    squares = jnp.zeros((TOK, 1), F32)
    for b in range(PLANES):
        summed = resid[:, b * HEADS : (b + 1) * HEADS].astype(F32) + heads_in[b].astype(F32)
        squares = squares + jnp.sum(summed * summed, axis=1, keepdims=True)
    scale = lax.rsqrt(squares / D + 1e-06)

    def summed_at(b):
        at = slice(b * CHUNK, (b + 1) * CHUNK)
        plane, first = b * CHUNK // HEADS, b * CHUNK % HEADS
        return resid[:, at].astype(F32) + heads_in[plane, :, first : first + CHUNK].astype(F32)

    for b in range(2 * CHUNKS):
        normed = summed_at(b) * scale * gain[:, b * CHUNK : (b + 1) * CHUNK]
        gath[b % CHUNKS, z, b // CHUNKS] = normed.astype(BF16)

    def piece(j, r, slot, half):
        some = pl.ds(LAPS[j][0], LAPS[j][1])
        return gath.at[some, slot] if r < 4 else gath.at[some, slot, half]

    def right(j, r):
        ref = piece(j, r, mod8(z - r + 1), 0)
        return send(ref, ref, r_s.at[0], r_r.at[j, r - 1], ctx, mod8(z + 1))

    def left(j, r):
        ref = piece(j, r, mod8(z + r - 1), 1)
        return send(ref, ref, l_s.at[0], l_r.at[j, r - 1], ctx, mod8(z - 1))

    def right_in(j, r):
        ref = piece(j, r, mod8(z - r), 0)
        return send(ref, ref, r_s.at[0], r_r.at[j, r - 1], ctx, mod8(z + 1))

    def left_in(j, r):
        ref = piece(j, r, mod8(z + r), 1)
        return send(ref, ref, l_s.at[0], l_r.at[j, r - 1], ctx, mod8(z - 1))

    def across(k):
        return send(gath.at[k, pl.ds(0, PLANES), 1 - c], toks.at[k, c], c_s.at[0], c_r.at[k], sibling, z)

    def across_in(k):
        ref = toks.at[k, 1 - c]
        return send(ref, ref, c_s.at[0], c_r.at[k], sibling, z)

    def arrived(k):
        across(k).start()
        toks[k, c] = gath[k, :, c]

    lot = pl.ds(0, SLOTS)

    def put(k, row, product):
        for i in range(GRID):
            kv[k * CHIPS + row * GRID + i, lot, :] = product[i * SLOTS : (i + 1) * SLOTS]

    mine_at = pl.ds(pl.multiple_of(chip * SLOTS, SLOTS), SLOTS)

    def d_send(k, d):
        return send(kv.at[k * CHIPS + d, lot, :], rows.at[mine_at, pl.ds(k * CHUNK, CHUNK)], d_s.at[0], d_r.at[x], d * 2 + c, z)

    def dispatch(k):
        across_in(k).wait_recv()

        def step(g):
            xd = lax.rem(x + g, GRID)
            slot = lax.broadcasted_iota(jnp.int32, (SLOTS, COLUMN), 0)
            for i in range(GRID):
                hot[i * SLOTS : (i + 1) * SLOTS, :] = jnp.where(slot.astype(F32) == pos_in[xd * GRID + i], 1.0, 0.0).astype(BF16)
            picked = jnp.dot(hot[...], toks[k].reshape(COLUMN, CHUNK), preferred_element_type=F32)
            put(k, xd, picked.astype(BF16))
            for j in range(1, GRID):
                d_send(k, xd * GRID + lax.rem(y + j, GRID)).start()

            @pl.when(g > 0)
            def _():
                d_send(k, xd * GRID + y).start()

        loop(GRID, step)
        rows[mine_at, k * CHUNK : (k + 1) * CHUNK] = kv[k * CHIPS + chip, lot, :]

    for tick in range(1, len(LAPS) + 5):
        for j, (first_k, count) in enumerate(LAPS):
            r = tick - j
            if 2 <= r <= 5:
                right_in(j, r - 1).wait_recv()
                left_in(j, r - 1).wait_recv()
            if 1 <= r <= 4:
                right(j, r).start()
                left(j, r).start()
            if r == 5:
                for k in range(first_k, first_k + count):
                    arrived(k)
        if tick in RING:
            next_piece(EARLY + RING.index(tick))
        if tick == len(LAPS) + 3:
            for p in range(EARLY + len(RING), PIECES):
                next_piece(p)
        for j, (first_k, count) in enumerate(LAPS):
            if tick - j == (5 if j in (0, len(LAPS) - 1) else 6):
                for k in range(first_k, first_k + count):
                    dispatch(k)

    lane = lax.broadcasted_iota(jnp.int32, (HEAD_SIZE, ROWS), 1)
    owner = lax.broadcasted_iota(jnp.int32, (HEAD_SIZE, ROWS), 0) * SLOTS
    spread = jnp.where((lane >= owner) & (lane < owner + SLOTS), 1.0, 0.0).astype(BF16)

    def build(b):
        at = pl.ds(pl.multiple_of(b * 128, 128), 128)
        slot = jnp.dot(pos_out[at, :], spread, preferred_element_type=F32)
        share = jnp.dot(share_out[at, :], spread, preferred_element_type=F32)
        want = lax.rem(lax.broadcasted_iota(jnp.int32, (128, ROWS), 1), SLOTS).astype(F32)
        comb[at, :] = jnp.where(slot == want, share, 0.0).astype(BF16)

    loop(COLUMN // 128, build)

    pltpu.make_async_copy(wout, wout, w_s.at[1]).wait()

    @pl.when(same)
    def _():
        pltpu.make_async_copy(w_own, win, w_s.at[0]).wait()

    def moved(kind):
        ref = win.at[pl.ds(0, HALF // 2), :]
        return send(ref, ref, x_s.at[kind], x_r.at[kind], ctx, z)

    @pl.when(apart)
    def _():
        moved(0).wait_recv()
        moved(2).wait_recv()

    def span_of(g):
        xs = lax.rem(x - g + GRID, GRID)
        return xs, pl.ds(pl.multiple_of(xs * GROUP, GROUP), GROUP)

    def p_send(g):
        _, at = span_of(g)
        return send(mine.at[at, :], theirs.at[at, :], p_s.at[0], p_r.at[g], sibling, z)

    def first(g):
        xs, at = span_of(g)

        def from_row(count):
            ref = rows.at[pl.ds(0, count), :]
            send(ref, ref, d_s.at[0], d_r.at[xs], ctx, z).wait_recv()

        @pl.when(g == 0)
        def _():
            from_row(GROUP - SLOTS)

        @pl.when(g > 0)
        def _():
            from_row(GROUP)

        mine[at, :] = jnp.dot(rows[at, :], win[...], preferred_element_type=F32).astype(BF16)
        p_send(g).start()

    def h_send(g):
        at = pl.ds(pl.multiple_of(span_of(g)[0] * GROUP, GROUP), GROUP // 2)
        return send(hid_out.at[at, :], hid.at[at, :], h_s.at[0], h_r.at[g], sibling, mate)

    def h_same(g):
        at = pl.ds(pl.multiple_of(span_of(g)[0] * GROUP + GROUP // 2, GROUP // 2), GROUP // 2)
        return send(hid.at[at, :], hid.at[at, :], h_s.at[0], h_r.at[g], ctx, mate)

    def hidden(g):
        p_send(g).wait_recv()
        xs, _ = span_of(g)

        def part(i):
            at = pl.ds(pl.multiple_of(xs * GROUP + i * 32, 32), 32)
            pre = mine[at, :].astype(F32) + theirs[at, :].astype(F32)
            gate, up = pre[:, :FF], pre[:, FF:]
            value = (gate / (1.0 + jnp.exp(-gate)) * up).astype(BF16)

            @pl.when(same)
            def _():
                hid[at, :] = value

            @pl.when(apart)
            def _():
                hid_out[at, :] = value

        loop(GROUP // 32, part)

        @pl.when(apart)
        def _():
            h_send(g).start()

        @pl.when(same)
        def _():
            h_same(g).start()

    def d_all(r_sem):
        ref = kv.at[pl.ds(0, CHUNKS * (CHIPS - 1)), lot, :]
        return send(ref, ref, d_s.at[0], r_sem, ctx, z)

    def o_send(n, d):
        return send(kv.at[n * CHIPS + d, lot, :], back.at[n, mine_at, :], o_s.at[0], o_r.at[n], d * 2 + c, z)

    def second(n, g):
        xs, at = span_of(g)

        @pl.when((n == 0) & apart)
        def _():
            send(hid.at[at, :], hid.at[at, :], h_s.at[0], h_r.at[g], sibling, mate).wait_recv()

        product = jnp.dot(hid[at, :], wout[n], preferred_element_type=F32).astype(BF16)
        put(n, xs, product)
        for j in range(1, GRID):
            o_send(n, xs * GRID + lax.rem(y + j, GRID)).start()

        @pl.when(g > 0)
        def _():
            o_send(n, xs * GRID + y).start()

        @pl.when(g == 0)
        def _():
            back[n, mine_at, :] = kv[n * CHIPS + chip, lot, :]

    def through(g):
        @pl.when(g < GRID)
        def _():
            first(g)

        @pl.when((g > 0) & (g < GRID + 1))
        def _():
            hidden(g - 1)

        @pl.when(g == 2)
        def _():
            d_all(d_r.at[0]).wait_send()

        @pl.when(g > 1)
        def _():
            second(0, g - 2)

    loop(GRID + 2, through)

    units = CHUNKS * 7 // 2 // 4
    for s_sem, r_sem in ((r_s, r_r), (l_s, l_r)):
        ref = gath.at[pl.ds(0, units), pl.ds(0, 4)]
        send(ref, ref, s_sem.at[0], r_sem.at[0, 0], ctx, z).wait_send()
    ref = gath.at[pl.ds(0, CHUNKS // 2)]
    send(ref, ref, c_s.at[0], c_r.at[0], ctx, z).wait_send()

    def u_send(n):
        return send(toks.at[n, 0], sib.at[n], u_s.at[0], u_r.at[n], sibling, z)

    def z_send(n, to):
        return send(gath.at[n, to, 0], parts.at[n, z], z_s.at[0], z_r.at[n], ctx, to)

    def combine(step):
        @pl.when((step > 0) & (step < CHUNKS))
        def _():
            loop(GRID, lambda g: second(step, g))

        @pl.when(step > 1)
        def _():
            n = step - 2

            ref = back.at[n, pl.ds(0, ROWS - SLOTS), :]
            send(ref, ref, o_s.at[0], o_r.at[n], ctx, z).wait_recv()
            total = jnp.dot(comb[tokens_of(1 - c), :], back[n], preferred_element_type=F32)
            toks[n, 0] = total.astype(BF16).reshape(PLANES, TOK, CHUNK)
            u_send(n).start()
            total = jnp.dot(comb[tokens_of(c), :], back[n], preferred_element_type=F32)
            u_send(n).wait_recv()
            total = (total + sib[n].reshape(SPAN, CHUNK).astype(F32)).astype(BF16)
            for s in range(PLANES):
                gath[n, s, 0] = total[s * TOK : (s + 1) * TOK]
            loop(PLANES - 1, lambda r: z_send(n, mod8(z + r + 1)).start())
            parts[n, z] = gath[n, z, 0]

        @pl.when(step > 3)
        def _():
            finish(step - 4)

    def finish(n):
        ref = parts.at[n, pl.ds(0, PLANES - 1)]
        send(ref, ref, z_s.at[0], z_r.at[n], ctx, z).wait_recv()
        for half in range(2):
            total = parts[n, half].astype(F32)
            for q in range(1, PLANES // 2):
                total = total + parts[n, 2 * q + half].astype(F32)
            at = pl.ds(pl.multiple_of((half * CHUNKS + n) * CHUNK, CHUNK), CHUNK)
            per_plane = HEADS // CHUNK
            within = pl.ds(pl.multiple_of(lax.rem(n, per_plane) * CHUNK, CHUNK), CHUNK)
            heads = heads_in[half * (PLANES // 2) + lax.div(n, per_plane), :, within]
            out[:, at] = (resid[:, at].astype(F32) + heads.astype(F32) + total).astype(BF16)

    loop(CHUNKS + 2, combine)
    loop(2, lambda i: finish(CHUNKS - 2 + i))

    send(mine, mine, p_s.at[0], p_r.at[0], ctx, z).wait_send()
    ref = hid.at[pl.ds(0, ROWS // 2), :]
    send(ref, ref, h_s.at[0], h_r.at[0], ctx, z).wait_send()
    ref = kv.at[pl.ds(0, CHUNKS * (CHIPS - 1)), lot, :]
    send(ref, ref, o_s.at[0], o_r.at[0], ctx, z).wait_send()
    ref = toks.at[pl.ds(0, CHUNKS), 0]
    send(ref, ref, u_s.at[0], u_r.at[0], ctx, z).wait_send()
    ref = parts.at[:, pl.ds(0, PLANES - 1)]
    send(ref, ref, z_s.at[0], z_r.at[0], ctx, z).wait_send()

    @pl.when(apart)
    def _():
        moved(0).wait_send()
        moved(1).wait_send()

    @pl.when(same)
    def _():
        moved(2).wait_send()


def run_layer(cols, offsets, own_kv, queries, ids, gates, resid, gain, w_own, w_out):
    vmem = pl.BlockSpec(memory_space=pltpu.VMEM)
    smem = pl.BlockSpec(memory_space=pltpu.SMEM)
    hbm = pl.BlockSpec(memory_space=pl.ANY)
    dma = pltpu.SemaphoreType.DMA
    out, _ = pl.pallas_call(
        layer_kernel,
        out_shape=(
            jax.ShapeDtypeStruct((TOK, D), BF16),
            jax.ShapeDtypeStruct((HALF // 2, 2 * FF), BF16),
        ),
        in_specs=[smem] * 2 + [vmem] * 6 + [hbm] * 2,
        out_specs=(vmem, hbm),
        scratch_shapes=[
            pltpu.VMEM((CHUNKS * CHIPS, BLOCK_TOKENS, CHUNK), BF16),
            pltpu.VMEM((TOK, HEAD_SIZE), F32),
            pltpu.VMEM((COLUMN, HEAD_SIZE), F32),
            pltpu.VMEM((CHIPS, 1, COLUMN), F32),
            pltpu.VMEM((COLUMN, HEAD_SIZE), BF16),
            pltpu.VMEM((COLUMN, HEAD_SIZE), BF16),
            pltpu.VMEM((PLANES, TOK, HEADS), BF16),
            pltpu.VMEM((CHUNKS, PLANES, 2, TOK, CHUNK), BF16),
            pltpu.VMEM((CHUNKS, 2, PLANES, TOK, CHUNK), BF16),
            pltpu.VMEM((GROUP, COLUMN), BF16),
            pltpu.VMEM((ROWS, HALF), BF16),
            pltpu.VMEM((HALF, 2 * FF), BF16),
            pltpu.VMEM((CHUNKS, FF, CHUNK), BF16),
            pltpu.VMEM((ROWS, 2 * FF), BF16),
            pltpu.VMEM((ROWS, 2 * FF), BF16),
            pltpu.VMEM((ROWS, FF), BF16),
            pltpu.VMEM((ROWS, FF), BF16),
            pltpu.VMEM((CHUNKS, ROWS, CHUNK), BF16),
            pltpu.VMEM((COLUMN, ROWS), BF16),
            pltpu.VMEM((CHUNKS, PLANES, TOK, CHUNK), BF16),
            pltpu.VMEM((CHUNKS, PLANES, TOK, CHUNK), BF16),
            dma((1,)), dma((CHIPS, SPAN // BLOCK_TOKENS)),
            dma((1,)), dma((1,)),
            dma((1,)),
            dma((1,)), dma((1,)),
            dma((2,)), dma((2,)),
            dma((1,)), dma((len(LAPS), 4)),
            dma((1,)), dma((len(LAPS), 4)),
            dma((1,)), dma((CHUNKS,)),
            dma((1,)), dma((GRID,)),
            dma((1,)), dma((GRID,)),
            dma((1,)), dma((GRID,)),
            dma((1,)), dma((CHUNKS,)),
            dma((1,)), dma((CHUNKS,)),
            dma((1,)), dma((CHUNKS,)),
            dma((2,)),
            dma((3,)), dma((3,)),
        ],
        compiler_params=pltpu.CompilerParams(
            collective_id=0, has_side_effects=True, vmem_limit_bytes=VMEM_BYTES
        ),
        cost_estimate=pl.CostEstimate(flops=25 * 10**9, bytes_accessed=12 * 10**6, transcendentals=10**6),
        name="layer",
    )(cols, offsets, own_kv, queries, ids, gates, resid, gain, w_own, w_out)
    return out


def local(
    queries, key_value_stack, vertical_cols, slash_offsets, resid,
    norm_gain, expert_ids, gate_weights, w_in, w_out,
):
    z = lax.axis_index("exp")
    heads_dev = queries.shape[1] // HEAD_SIZE
    kv_head = z * heads_dev // (QUERY_HEADS // KEY_VALUE_HEADS)
    own_kv = lax.dynamic_slice_in_dim(key_value_stack, kv_head * HEAD_SIZE, HEAD_SIZE, 2)
    own_kv = own_kv.reshape(-1, BLOCK_TOKENS, 2 * HEAD_SIZE)
    return run_layer(
        vertical_cols.T, slash_offsets.T, own_kv, queries, expert_ids.T, gate_weights.T,
        resid, norm_gain[None, :], w_in[0], w_out[0],
    )


def solution(mesh):
    in_specs = (
        P("ctx", "exp"),
        P("ctx", None, None),
        P(),
        P(),
        P(("ctx", "exp"), None),
        P(),
        P(("ctx", "exp"), None),
        P(("ctx", "exp"), None),
        P(("ctx", "exp"), None, None),
        P(("ctx", "exp"), None, None),
    )
    out_specs = P(("ctx", "exp"), None)
    return jax.shard_map(local, mesh=mesh, in_specs=in_specs, out_specs=out_specs, check_vma=False)
```

time: 349 us -> 240 us (0.69)
  blocking collectives: 83.3 us -> 0 us
  between operations: 13.5 us -> 0.01 us
  Pallas kernels: 223 us -> 236 us
  starting transfers between devices: 11.5 us -> 0 us
  local copies, waits for them, and re-layouts: 12.5 us -> 3.87 us
  other arithmetic: 4.11 us -> 0 us
    all_gather x1 -> x0, blocking collectives: 83.3 us -> none  [local(): routing = lax.all_gather(routing, 'exp', axis=0, tiled=True)]
    pallas_call x2 -> x1, Pallas kernels: 223 us -> 236 us  [run_layer(): pl.pallas_call(layer_kernel, out_shape=(jax.ShapeDtypeStruct((TOK, D), BF...]
    ppermute x2 -> x0, starting transfers between devices: 11.5 us -> none  [the longest x1 6.51 us: local(): other = lax.ppermute(routing, 'ctx', [(i, i ^ 1) for i in range(n_ctx)])]
    unnamed x14 -> x1, local copies, waits for them, and re-layouts: 7.89 us -> 1.87 us
  transfers between devices with their start and end apart: 3 -> 0, of which waited for: 0 -> 0; matrix products, arithmetic and copies ran while one was open for 2% -> 0% of each run, Pallas kernels for 2% -> 0%
where the time goes in v3:
time: 240 us
  Pallas kernels  236 us (98%)
  local copies, waits for them, and re-layouts  3.87 us (2%)
    pallas_call x1, Pallas kernels, run_layer(): pl.pallas_call(layer_kernel, out_shape=(jax.ShapeDtypeStruct((TOK, D), BF...  236 us

profile of v3, /device:TPU:1, one launch (start us, length us, event | category | flops | bytes accessed | tf_op | source)
XLA Modules:
  0.0 240.0 jit_solution(9795894013437954422)
XLA Ops:
  0.0 1.1 constant_dynamic-slice_fusion
  1.1 0.9 reshape.3.own
  2.0 236.1 %layer.1 = (bf16[64,4096]{1,0:T(8,128)(2,1)}, bf16[1024,1536]{1,0:T(8,128)(2,1)}) custom-call(s32[4,128]{1,0:T(4,128)} %bitcast.12, s32[2,128]{1,0:T(2,128)} %bitcast.13, bf16[4,128,256]{2,1,0:T(8,128)(2,1)} %reshape.3.own, bf16[512,512]{1,0:T(8,128)(2,1)} %queries.1, s32[8,64]{1,0:T(8,128)} %bitcast.10, f32[8,64]{1,0:T(8,128)} %bitcast.11, ...), custom_call_target="tpu_custom_call" | custom-call | flops 24999999488 | bytes 12000000 | tf_op jit(solution)/shard_map/layer/pallas_call | solution.py:660
  238.1 1.9 copy.12

commit v4 on v3

--- a/solution.py
+++ b/solution.py
@@ -595,9 +595,9 @@
         def _():
             loop(GRID, lambda g: second(step, g))
 
-        @pl.when(step > 1)
-        def _():
-            n = step - 2
+        @pl.when(step > 2)
+        def _():
+            n = step - 3
 
             ref = back.at[n, pl.ds(0, ROWS - SLOTS), :]
             send(ref, ref, o_s.at[0], o_r.at[n], ctx, z).wait_recv()
@@ -612,9 +612,9 @@
             loop(PLANES - 1, lambda r: z_send(n, mod8(z + r + 1)).start())
             parts[n, z] = gath[n, z, 0]
 
-        @pl.when(step > 3)
-        def _():
-            finish(step - 4)
+        @pl.when(step > 4)
+        def _():
+            finish(step - 5)
 
     def finish(n):
         ref = parts.at[n, pl.ds(0, PLANES - 1)]
@@ -629,7 +629,7 @@
             heads = heads_in[half * (PLANES // 2) + lax.div(n, per_plane), :, within]
             out[:, at] = (resid[:, at].astype(F32) + heads.astype(F32) + total).astype(BF16)
 
-    loop(CHUNKS + 2, combine)
+    loop(CHUNKS + 3, combine)
     loop(2, lambda i: finish(CHUNKS - 2 + i))
 
     send(mine, mine, p_s.at[0], p_r.at[0], ctx, z).wait_send()

time: 240 us -> 244 us (1.017)
  Pallas kernels: 236 us -> 240 us
    pallas_call x1, Pallas kernels: 236 us -> 240 us  [run_layer(): pl.pallas_call(layer_kernel, out_shape=(jax.ShapeDtypeStruct((TOK, D), BF...]
where the time goes in v4:
time: 244 us; the launch traced here: 243 us
  Pallas kernels  240 us (98%)
  local copies, waits for them, and re-layouts  3.87 us (2%)
    pallas_call x1, Pallas kernels, run_layer(): pl.pallas_call(layer_kernel, out_shape=(jax.ShapeDtypeStruct((TOK, D), BF...  240 us

profile of v4, /device:TPU:1, one launch (start us, length us, event | category | flops | bytes accessed | tf_op | source)
XLA Modules:
  0.0 243.5 jit_solution(2272318006223351312)
XLA Ops:
  0.0 1.1 constant_dynamic-slice_fusion
  1.1 0.9 reshape.3.own
  2.0 239.6 %layer.1 = (bf16[64,4096]{1,0:T(8,128)(2,1)}, bf16[1024,1536]{1,0:T(8,128)(2,1)}) custom-call(s32[4,128]{1,0:T(4,128)} %bitcast.12, s32[2,128]{1,0:T(2,128)} %bitcast.13, bf16[4,128,256]{2,1,0:T(8,128)(2,1)} %reshape.3.own, bf16[512,512]{1,0:T(8,128)(2,1)} %queries.1, s32[8,64]{1,0:T(8,128)} %bitcast.10, f32[8,64]{1,0:T(8,128)} %bitcast.11, ...), custom_call_target="tpu_custom_call" | custom-call | flops 24999999488 | bytes 12000000 | tf_op jit(solution)/shard_map/layer/pallas_call | solution.py:660
  241.6 1.9 copy.12
